TPU v7x, 512 devices: a whole 4x8x8 slice. The times are simulated.
512 devices in a mesh: tm: 64 (over z, y), kv: 8 (over x, core).
Axes of the slice: x: 4, y: 8, z: 8, core: 2. Of those that a mesh axis runs over, the one named last changes fastest.
Arguments:
- frames: bfloat16 [12288, 512], P(('tm', 'kv')), may hold values from -6 to 6
- attn_gain: float32 [512], replicated, may hold values from 0.5 to 2
- w_query: bfloat16 [512, 512], replicated, may hold values from -14 to 14
- w_key: bfloat16 [512, 512], replicated, may hold values from -1 to 1
- w_value: bfloat16 [512, 512], replicated, may hold values from -0.25 to 0.25
- w_out: bfloat16 [512, 512], replicated, may hold values from -0.25 to 0.25
- conv_gain: float32 [512], replicated, may hold values from 0.5 to 2
- w_expand: bfloat16 [512, 1024], replicated, may hold values from -0.25 to 0.25
- kernel: float32 [31, 512], replicated, may hold values from -1 to 1
- bn_scale: float32 [512], replicated, may hold values from 0.5 to 2
- bn_shift: float32 [512], replicated, may hold values from -3 to 3
- w_project: bfloat16 [512, 512], replicated, may hold values from -0.25 to 0.25
Outputs:
- attended: bfloat16 [12288, 512], P(('tm', 'kv'))
- layer_out: bfloat16 [12288, 512], P(('tm', 'kv'))
All inputs are finite; a program needn't handle non-finite values.
Results may differ from a plain program's by a relative error of at most 0.02.
Values may be sent and summed in bfloat16 or wider, within the bound.
A program may use at most 64 MiB of HBM per device.

v0:
```python
import jax
import jax.numpy as jnp
from jax import lax
from jax.sharding import PartitionSpec as P

HEADS = 8
HEAD_DIM = 64


def merged_2(x, axis, combine):
    everything = jax.tree.map(lambda part: lax.all_gather(part, axis), x)
    first = jax.tree.map(lambda part: part[0], everything)

    def turn(k, so_far):
        return combine(so_far, jax.tree.map(lambda part: part[k], everything))

    return lax.fori_loop(1, lax.axis_size(axis), turn, first)


def extended(cells, sides, width):
    for axis, dim in sides:
        count = lax.axis_size(axis)
        ends = count - 1
        head = lax.slice_in_dim(cells, 0, width, axis=dim)
        tail = lax.slice_in_dim(cells, cells.shape[dim] - width, cells.shape[dim], axis=dim)
        cells = jnp.concatenate(
            [
                lax.ppermute(tail, axis, [(i, (i + 1) % count) for i in range(ends)]),
                cells,
                lax.ppermute(head, axis, [((i + 1) % count, i) for i in range(ends)]),
            ],
            axis=dim,
        )
    return cells


def layer_norm(values, gain):
    mean = jnp.mean(values, axis=-1, keepdims=True)
    centered = values - mean
    var = jnp.mean(centered * centered, axis=-1, keepdims=True)
    return centered / jnp.sqrt(var + 1e-05) * gain


def rotate(heads_in, positions):
    half = HEAD_DIM // 2
    inverse = 10000.0 ** (-(jnp.arange(half, dtype=jnp.float32) * 2.0) / HEAD_DIM)
    angle = positions.astype(jnp.float32)[:, None] * inverse[None, :]
    cosine = jnp.cos(angle)[:, None, :]
    sine = jnp.sin(angle)[:, None, :]
    first = heads_in[..., :half]
    second = heads_in[..., half:]
    return jnp.concatenate(
        [first * cosine - second * sine, second * cosine + first * sine], axis=-1
    )


def absorb(carry, queries, keys, values):
    top_seen, total, weighted = carry
    count = keys.shape[0]
    for begin in range(0, count, 512):
        key_block = keys[begin : begin + 512]
        value_block = values[begin : begin + 512]
        score = jnp.einsum("qhd,khd->qhk", queries, key_block, preferred_element_type=jnp.float32)
        newest = jnp.maximum(top_seen, jnp.max(score, axis=-1))
        fade = jnp.exp(top_seen - newest)
        weight = jnp.exp(score - newest[:, :, None])
        total = total * fade + jnp.sum(weight, axis=-1)
        mixed = jnp.einsum(
            "qhk,khd->qhd",
            weight.astype(jnp.bfloat16),
            value_block,
            preferred_element_type=jnp.float32,
        )
        weighted = weighted * jnp.repeat(fade, HEAD_DIM, axis=1) + mixed.reshape(mixed.shape[0], -1)
        top_seen = newest
    return (top_seen, total, weighted)


def combine(first, second):
    newest = jnp.maximum(first[0], second[0])
    fade_one = jnp.exp(first[0] - newest)
    fade_two = jnp.exp(second[0] - newest)
    total = first[1] * fade_one + second[1] * fade_two
    weighted = first[2] * jnp.repeat(fade_one, HEAD_DIM, axis=1) + second[2] * jnp.repeat(
        fade_two, HEAD_DIM, axis=1
    )
    return (newest, total, weighted)


def on_device(
    frames,
    attn_gain,
    w_query,
    w_key,
    w_value,
    w_out,
    conv_gain,
    w_expand,
    kernel,
    bn_scale,
    bn_shift,
    w_project,
):
    rows = frames.shape[0]
    groups = lax.axis_size("kv")
    group = lax.axis_index("kv")
    first_row = (lax.axis_index("tm") * groups + group) * rows
    positions = first_row + jnp.arange(rows, dtype=jnp.int32)
    inputs = frames.astype(jnp.float32)
    normed = layer_norm(inputs, attn_gain).astype(jnp.bfloat16)
    q_local = jnp.dot(normed, w_query, preferred_element_type=jnp.float32).reshape(
        rows, HEADS, HEAD_DIM
    )
    q_local = (
        (rotate(q_local, positions) * 0.125).astype(jnp.bfloat16).reshape(rows, HEADS * HEAD_DIM)
    )
    queries = lax.all_gather(q_local, "kv", axis=0, tiled=True)
    query_rows = queries.shape[0]
    queries = queries.reshape(query_rows, HEADS, HEAD_DIM)
    start_state = (
        jnp.full((query_rows, HEADS), -1e30, jnp.float32),
        jnp.zeros((query_rows, HEADS), jnp.float32),
        jnp.zeros((query_rows, HEADS * HEAD_DIM), jnp.float32),
    )
    k_local = jnp.dot(normed, w_key, preferred_element_type=jnp.float32).reshape(
        rows, HEADS, HEAD_DIM
    )
    k_local = rotate(k_local, positions).astype(jnp.bfloat16).reshape(rows, HEADS * HEAD_DIM)
    v_local = jnp.dot(normed, w_value, preferred_element_type=jnp.float32).astype(jnp.bfloat16)
    pieces = (
        lax.all_gather(k_local, "tm", axis=0, tiled=True),
        lax.all_gather(v_local, "tm", axis=0, tiled=True),
    )
    count = pieces[0].shape[0]
    parts = absorb(
        start_state,
        queries,
        pieces[0].reshape(count, HEADS, HEAD_DIM),
        pieces[1].reshape(count, HEADS, HEAD_DIM),
    )
    merged = merged_2(parts, "kv", combine)
    own_total = lax.dynamic_slice_in_dim(merged[1], group * rows, rows, 0)
    own_weighted = lax.dynamic_slice_in_dim(merged[2], group * rows, rows, 0)
    context = (own_weighted / jnp.repeat(own_total, HEAD_DIM, axis=1)).astype(jnp.bfloat16)
    attended = jnp.dot(context, w_out, preferred_element_type=jnp.float32).astype(jnp.bfloat16)
    mid = inputs + lax.optimization_barrier(attended).astype(jnp.float32)
    conv_in = layer_norm(mid, conv_gain).astype(jnp.bfloat16)
    expanded = jnp.dot(conv_in, w_expand, preferred_element_type=jnp.float32)
    width = expanded.shape[1] // 2
    glu = (expanded[:, :width] * jax.nn.sigmoid(expanded[:, width:])).astype(jnp.bfloat16)
    half_width = (kernel.shape[0] - 1) // 2
    padded = extended(glu, ((("tm", "kv"), 0),), half_width)
    depth = jnp.zeros((rows, width), jnp.float32)
    for tap in range(kernel.shape[0]):
        depth = depth + kernel[tap][None, :] * padded[tap : tap + rows]
    act = jax.nn.silu(depth * bn_scale + bn_shift).astype(jnp.bfloat16)
    layer_out = (mid + jnp.dot(act, w_project, preferred_element_type=jnp.float32)).astype(
        jnp.bfloat16
    )
    return (attended, layer_out)


def solution(mesh):
    return jax.shard_map(
        on_device,
        mesh=mesh,
        in_specs=(P(("tm", "kv"), None), P(), P(), P(), P(), P(), P(), P(), P(), P(), P(), P()),
        out_specs=(P(("tm", "kv"), None), P(("tm", "kv"), None)),
        check_vma=False,
    )
```

profile of v0, /device:TPU:1, one launch (start us, length us, event | category | flops | bytes accessed | tf_op | source)
XLA Modules:
  0.0 260.5 jit_solution(7133495247157464174)
XLA Ops:
  7.2 0.9 convert_reduce_fusion
  8.2 0.9 fusion.50
  9.1 1.9 convolution_convert_fusion.1
  11.1 1.3 fusion.166
  12.5 1.3 fusion.164
  13.9 0.1 multiply_cosine_fusion
  14.0 0.1 multiply_subtract_fusion
  14.3 0.7 convert_element_type.155
  15.3 19.5 %all_gather.22 = bf16[192,512]{1,0:T(8,128)(2,1)S(1)} all-gather(bf16[24,512]{1,0:T(8,128)(2,1)S(1)} %convert_element_type.157), channel_id=1, replica_groups=mesh['tm'=64,'kv'=8] {'kv'}, dimensions={0}, use_global_device_ids=true | all-gather | bytes 221184 | tf_op jit(solution)/shard_map/all_gather | solution.py:117
  34.8 0.1 copy.29
  34.9 60.9 %all-gather.6.cloned.1.call-done = bf16[1536,512]{1,0:T(8,128)(2,1)} async-done(((bf16[24,512]{1,0:T(8,128)(2,1)}), bf16[1536,512]{1,0:T(8,128)(2,1)}) %all-gather.6.cloned.1.call-update) | async-done | bytes 1572880 | tf_op jit(solution)/shard_map/all_gather | solution.py:132
  95.8 2.5 fusion.170
  98.3 0.2 copy.34
  98.5 80.7 %all-gather.4.cloned.1.call-done = bf16[1536,512]{1,0:T(8,128)(2,1)} async-done(((bf16[24,512]{1,0:T(8,128)(2,1)}), bf16[1536,512]{1,0:T(8,128)(2,1)}) %all-gather.4.cloned.1.call-update) | async-done | bytes 1572880 | tf_op jit(solution)/shard_map/all_gather | solution.py:131
  179.2 2.3 fusion.171
  181.5 0.2 copy.28
  181.8 1.3 copy.31
  183.0 1.0 copy.30
  184.0 1.3 copy.33
  185.3 2.1 copy.32
  187.4 1.8 bitcast_reduce_fusion.1
  189.1 0.7 bitcast_reduce_fusion
  189.9 0.7 bitcast_reduce_fusion.2
  190.6 1.1 fusion.42
  191.7 1.1 fusion.39
  192.9 0.8 fusion.36
  193.7 1.0 copy.35
  194.7 2.8 %fusion.7 = f32[192,8]{0,1:T(8,128)S(1)} fusion(f32[8,512,192]{1,2,0:T(8,128)} %copy-done.4, f32[192,8]{0,1:T(8,128)S(1)} %get-tuple-element.258), kind=kLoop, calls=%fused_computation.20 | loop fusion | flops 1571328 | bytes 3158016 | tf_op jit(solution)/shard_map/reduce_sum | solution.py:67
  197.5 3.0 %fusion.9 = (f32[192,8]{0,1:T(8,128)S(1)}, f32[192,8]{0,1:T(8,128)S(1)}) fusion(f32[8,512,192]{1,2,0:T(8,128)S(1)} %copy-done.2, f32[192,8]{0,1:T(8,128)S(1)} %get-tuple-element.208, f32[192,8]{0,1:T(8,128)S(1)} %get-tuple-element.207, f32[8,512,192]{1,2,0:T(8,128)} %copy-done.3), kind=kLoop, calls=%fused_computation.22 | loop fusion | flops 3142656 | bytes 6316032 | tf_op jit(solution)/shard_map/reduce_sum | solution.py:67
  200.6 17.6 %all_gather.24 = f32[8,192,8]{1,2,0:T(8,128)S(1)} all-gather(f32[1,192,8]{1,2,0:T(8,128)S(1)} %get-tuple-element.252), channel_id=1, replica_groups=mesh['tm'=64,'kv'=8] {'kv'}, dimensions={0}, use_global_device_ids=true | all-gather | bytes 55296 | tf_op jit(solution)/shard_map/all_gather | solution.py:11
  218.2 12.8 %all_gather.23 = f32[8,192,8]{1,2,0:T(8,128)S(1)} all-gather(f32[1,192,8]{1,2,0:T(8,128)S(1)} %get-tuple-element.253), channel_id=1, replica_groups=mesh['tm'=64,'kv'=8] {'kv'}, dimensions={0}, use_global_device_ids=true | all-gather | bytes 55296 | tf_op jit(solution)/shard_map/all_gather | solution.py:11
  231.0 1.0 slice_bitcast_fusion
  232.0 0.2 copy.36
  232.3 10.5 %while.19 = (s32[]{:T(128)}, f32[192,8]{0,1:T(8,128)S(1)}, f32[192,8]{0,1:T(8,128)S(1)}, f32[192,512]{0,1:T(8,128)S(1)}, f32[8,192,8]{1,2,0:T(8,128)S(1)}, /*ind...) while((s32[]{:T(128)}, f32[192,8]{0,1:T(8,128)S(1)}, ...), condition=%wide.region_9.0_spmd, body=%wide.region_8.0_spmd.sunk | while | flops 304133 | bytes 2814095 | solution.py:17
  232.3 1.1 constant_dynamic-slice_fusion.3
  233.4 0.2 copy.40
  233.6 0.2 fusion.194
  233.9 1.0 constant_dynamic-slice_fusion.3
  234.9 0.2 copy.40
  235.1 0.2 fusion.194
  235.4 1.0 constant_dynamic-slice_fusion.3
  236.4 0.2 copy.40
  236.6 0.2 fusion.194
  236.9 1.0 constant_dynamic-slice_fusion.3
  237.9 0.2 copy.40
  238.1 0.2 fusion.194
  238.4 1.0 constant_dynamic-slice_fusion.3
  239.4 0.2 copy.40
  239.6 0.2 fusion.194
  239.9 1.0 constant_dynamic-slice_fusion.3
  240.9 0.2 copy.40
  241.1 0.2 fusion.194
  241.3 1.0 constant_dynamic-slice_fusion.3
  242.4 0.2 copy.40
  242.6 0.2 fusion.194
  242.9 0.1 fusion.46
  243.0 0.2 convolution_convert_fusion
  243.3 0.1 fusion.58
  243.4 0.2 multiply_reduce_fusion
  243.6 0.3 fusion.59
  243.9 2.9 %collective-permute-start = (bf16[15,512]{1,0:T(8,128)(2,1)S(1)}, bf16[15,512]{1,0:T(8,128)(2,1)S(1)}, u32[]{:S(2)}, u32[]{:S(2)}) collective-permute-start(bf16[15,512]{1,0:T(8,128)(2,1)S(1)} %get-tuple-element.250), channel_id=1, source_target_pairs={{0,1},{1,2},{2,3},{3,4},{4,5},{5,6},{6,7},{7,8},{8,9},{9,10},{10,1... | collective-permute-start | bytes 46088 | tf_op jit(solution)/shard_map/ppermute | solution.py:28
  246.8 1.9 collective-permute-start.1
  248.8 3.1 %collective-permute-done.1 = bf16[15,512]{1,0:T(8,128)(2,1)S(1)} collective-permute-done((bf16[15,512]{1,0:T(8,128)(2,1)S(1)}, bf16[15,512]{1,0:T(8,128)(2,1)S(1)}, u32[]{:S(2)}, u32[]{:S(2)}) %collective-permute-start.1) | collective-permute-done | bytes 15392 | tf_op jit(solution)/shard_map/ppermute | solution.py:30
  251.9 2.1 fusion.45
  (62 shorter events, 1.1 us)
Async XLA Ops:
  7.2 236.4 %copy-start = (bf16[512,1024]{1,0:T(8,128)(2,1)S(1)}, bf16[512,1024]{1,0:T(8,128)(2,1)}, u32[]{:S(2)}) copy-start(bf16[512,1024]{1,0:T(8,128)(2,1)} %param.21) | copy-start | bytes 3145732
  7.2 88.6 %all-gather.6.cloned.1.call-start = ((), (), s32[]{:S(2)}) async-start(), calls=%async_computation.1 | async-start | bytes 1597440 | tf_op jit(solution)/shard_map/all_gather | solution.py:132
  11.1 168.2 %all-gather.4.cloned.1.call-start = ((), (), s32[]{:S(2)}) async-start(), calls=%async_computation | async-start | bytes 1597440 | tf_op jit(solution)/shard_map/all_gather | solution.py:131
  15.0 216.0 %all-gather.8.cloned.1.call-start = ((), (), s32[]{:S(2)}) async-start(), calls=%async_computation.2 | async-start | bytes 3538944 | tf_op jit(solution)/shard_map/all_gather | solution.py:11
  189.1 2.6 %copy-start.1 = (f32[8,512,192]{1,2,0:T(8,128)}, f32[8,512,192]{1,2,0:T(8,128)S(1)}, u32[]{:S(2)}) copy-start(f32[8,512,192]{1,2,0:T(8,128)S(1)} %get-tuple-element.264) | copy-start | bytes 9437188
  189.1 1.5 copy-start.5
  189.9 3.0 %copy-start.3 = (f32[8,512,192]{1,2,0:T(8,128)}, f32[8,512,192]{1,2,0:T(8,128)S(1)}, u32[]{:S(2)}) copy-start(f32[8,512,192]{1,2,0:T(8,128)S(1)} %get-tuple-element.262) | copy-start | bytes 9437188
  190.6 2.2 copy-start.4
  192.8 1.8 copy-start.9
  194.7 2.9 %copy-start.2 = (f32[8,512,192]{1,2,0:T(8,128)S(1)}, f32[8,512,192]{1,2,0:T(8,128)}, u32[]{:S(2)}) copy-start(f32[8,512,192]{1,2,0:T(8,128)} %copy-done.1) | copy-start | bytes 9437188
  232.2 10.8 %copy-start.7 = (bf16[512,512]{1,0:T(8,128)(2,1)S(1)}, bf16[512,512]{1,0:T(8,128)(2,1)}, u32[]{:S(2)}) copy-start(bf16[512,512]{1,0:T(8,128)(2,1)} %param.19) | copy-start | bytes 1572868
  232.2 11.0 %copy-start.6 = (bf16[24,512]{1,0:T(8,128)(2,1)S(1)}, bf16[24,512]{1,0:T(8,128)(2,1)}, u32[]{:S(2)}) copy-start(bf16[24,512]{1,0:T(8,128)(2,1)} %param.14) | copy-start | bytes 73732
  232.2 11.4 %copy-start.10 = (f32[512]{0:T(512)S(1)}, f32[512]{0:T(512)}, u32[]{:S(2)}) copy-start(f32[512]{0:T(512)} %param.20) | copy-start | bytes 6148
  232.3 19.6 %copy-start.11 = (f32[512]{0:T(512)S(1)}, f32[512]{0:T(512)}, u32[]{:S(2)}) copy-start(f32[512]{0:T(512)} %param.24) | copy-start | bytes 6148
  232.3 19.6 %copy-start.12 = (f32[512]{0:T(512)S(1)}, f32[512]{0:T(512)}, u32[]{:S(2)}) copy-start(f32[512]{0:T(512)} %param.23) | copy-start | bytes 6148
  243.2 10.7 %copy-start.8 = (bf16[24,512]{1,0:T(8,128)(2,1)}, bf16[24,512]{1,0:T(8,128)(2,1)S(1)}, u32[]{:S(2)}) copy-start(bf16[24,512]{1,0:T(8,128)(2,1)S(1)} %convolution_convert_fusion) | copy-start | bytes 73732
  243.9 4.8 %collective-permute-start = (bf16[15,512]{1,0:T(8,128)(2,1)S(1)}, bf16[15,512]{1,0:T(8,128)(2,1)S(1)}, u32[]{:S(2)}, u32[]{:S(2)}) collective-permute-start(bf16[15,512]{1,0:T(8,128)(2,1)S(1)} %get-tuple-element.250), channel_id=1, source_target_pairs={{0,1},{1,2},{2,3},{3,4},{4,5},{5,6},{6,7},{7,8},{8,9},{9,10},{10,1... | collective-permute-start | bytes 46088 | tf_op jit(solution)/shard_map/ppermute | solution.py:28
  246.8 5.1 %collective-permute-start.1 = (bf16[15,512]{1,0:T(8,128)(2,1)S(1)}, bf16[15,512]{1,0:T(8,128)(2,1)S(1)}, u32[]{:S(2)}, u32[]{:S(2)}) collective-permute-start(bf16[15,512]{1,0:T(8,128)(2,1)S(1)} %get-tuple-element.251), channel_id=1, source_target_pairs={{1,0},{2,1},{3,2},{4,3},{5,4},{6,5},{7,6},{8,7},{9,8},{10,9},{11,1... | collective-permute-start | bytes 46088 | tf_op jit(solution)/shard_map/ppermute | solution.py:30
Sparse Core Ops, SparseCore 0:
  11.6 84.1 all-gather.5
  99.4 79.7 all-gather.3
  194.8 34.8 all-gather.7
where the time goes:
time: 264 us; the launch traced here: 261 us
  waiting for transfers between devices  145 us (55%)
  blocking collectives  49.9 us (19%)
  local copies, waits for them, and re-layouts  22.9 us (9%)
  between operations  14.1 us (5%)
  matrix products  13.3 us (5%)
  other arithmetic  10.3 us (4%)
  starting transfers between devices  4.91 us (2%)
    all_gather x1, waiting for transfers between devices, on_device(): lax.all_gather(k_local, 'tm', axis=0, tiled=True)  80.7 us
    all_gather x1, waiting for transfers between devices, on_device(): lax.all_gather(v_local, 'tm', axis=0, tiled=True)  60.9 us
    all_gather x2, blocking collectives, merged_2(): everything = jax.tree.map(lambda part: lax.all_gather(part, axis), x)  30.4 us
    all_gather x1, blocking collectives, on_device(): queries = lax.all_gather(q_local, 'kv', axis=0, tiled=True)  19.5 us
    dynamic_slice x14, local copies, waits for them, and re-layouts, turn(): return combine(so_far, jax.tree.map(lambda part: part[k], everything))  8.63 us
    slice x4, local copies, waits for them, and re-layouts, absorb(): value_block = values[begin:begin + 512]  5.99 us
    reduce_sum x2, other arithmetic, absorb(): total = total * fade + jnp.sum(weight, axis=-1)  5.81 us
  transfers between devices with their start and end apart: 5, of which 3 were waited for; matrix products, arithmetic and copies ran while one was open for 5% of the time, Pallas kernels for 0%

commit v1 on v0

v1 whole, which is shorter than its diff:
```python
import functools
import math

import jax
import jax.numpy as jnp
from jax import lax
from jax.experimental import pallas as pl
from jax.experimental.pallas import tpu as pltpu
from jax.sharding import PartitionSpec as P

HEAD_DIM = 64
HALF = HEAD_DIM // 2
LANES = 128
HALO = 16
WINDOW = 64
MESH = pl.DeviceIdType.MESH
BF16 = jnp.bfloat16
F32 = jnp.float32


def layer_norm(values, gain):
    mean = jnp.mean(values, axis=-1, keepdims=True)
    centered = values - mean
    var = jnp.mean(centered * centered, axis=-1, keepdims=True)
    return centered / jnp.sqrt(var + 1e-05) * gain


def matmul(a, b):
    return jnp.dot(a, b, preferred_element_type=F32)


def folded(rows):
    half = rows.shape[0] // 2
    lane = lax.broadcasted_iota(jnp.int32, (half, LANES), 1)
    return jnp.where(lane < HEAD_DIM, pltpu.roll(rows[:half], HEAD_DIM, 1), rows[half:]).astype(BF16)


def all_heads(ref):
    columns = []
    lane = lax.broadcasted_iota(jnp.int32, ref.shape[1:], 1)
    for pair in range(ref.shape[0] // 2):
        even = ref[2 * pair].astype(F32)
        odd = ref[2 * pair + 1].astype(F32)
        top = jnp.where(lane < HEAD_DIM, even, pltpu.roll(odd, HEAD_DIM, 1))
        bottom = jnp.where(lane < HEAD_DIM, pltpu.roll(even, HEAD_DIM, 1), odd)
        columns.append(jnp.concatenate([top, bottom], axis=0))
    return jnp.concatenate(columns, axis=1)


def layer_kernel(
    side,
    frames_hbm,
    attn_gain_hbm,
    conv_gain_hbm,
    taps_hbm,
    scale_hbm,
    shift_hbm,
    w_query_hbm,
    w_key_hbm,
    w_value_hbm,
    w_out_hbm,
    w_expand_hbm,
    w_project_hbm,
    attended_hbm,
    layer_hbm,
    attended_ref,
    layer_ref,
    frames_ref,
    attn_gain_ref,
    conv_gain_ref,
    taps_ref,
    scale_ref,
    shift_ref,
    w_query,
    w_key,
    w_value,
    w_out,
    w_expand,
    w_project,
    head_send,
    head_recv,
    kv_all,
    kv_wide,
    q_all,
    part_send,
    part_recv,
    ctx_send,
    ctx_recv,
    edge_send,
    edge_recv,
    context,
    halo_send,
    halo_recv,
    padded,
    load_sem,
    store_sem,
    head_ssem,
    head_rsem,
    kv_ssem,
    kv_rsem,
    q_ssem,
    q_rsem,
    part_ssem,
    part_rsem,
    ctx_ssem,
    ctx_rsem,
    edge_ssem,
    edge_rsem,
    halo_ssem,
    halo_rsem,
):
    rows, width = frames_ref.shape
    groups = head_send.shape[0]
    block = rows * groups
    half_block = block // 2
    blocks = side * side
    tm = lax.axis_index("tm")
    kv = lax.axis_index("kv")
    core = kv % 2
    slow = tm // side
    fast = tm % side
    key_at = fast + core * (slow - fast)
    key_stride = 1 + core * (side - 1)
    query_at = slow + core * (fast - slow)
    query_stride = side - core * (side - 1)

    def kv_peer(d):
        return (tm, (kv + d) % groups)

    def key_peer(d):
        return (tm + ((key_at + d) % side - key_at) * key_stride, kv)

    def query_peer(d):
        return (tm + ((query_at + d) % side - query_at) * query_stride, kv)

    devices = groups * blocks
    me = tm * groups + kv
    following = (me + 1) % devices
    preceding = (me + devices - 1) % devices
    following = (following // groups, following % groups)
    preceding = (preceding // groups, preceding % groups)
    later = (tm + 1) % blocks
    earlier = (tm + blocks - 1) % blocks
    near = sorted(range(1, side), key=lambda d: min(d, side - d))

    def greet(device):
        pl.semaphore_signal(barrier, inc=1, device_id=device, device_id_type=MESH)

    loads = [
        pltpu.make_async_copy(source, target, load_sem.at[i])
        for i, (source, target) in enumerate(
            (
                (frames_hbm, frames_ref),
                (attn_gain_hbm, attn_gain_ref),
                (w_key_hbm, w_key),
                (w_value_hbm, w_value),
                (w_query_hbm, w_query),
                (w_out_hbm, w_out),
                (conv_gain_hbm, conv_gain_ref),
                (w_expand_hbm, w_expand),
                (taps_hbm, taps_ref),
                (scale_hbm, scale_ref),
                (shift_hbm, shift_ref),
                (w_project_hbm, w_project),
            )
        )
    ]
    for load in loads[:5]:
        load.start()

    barrier = pltpu.get_barrier_semaphore()
    for d in range(1, groups):
        greet(kv_peer(d))
    for d in range(1, side):
        greet(key_peer(d))
        greet(query_peer(d))

    @pl.when(kv == groups - 1)
    def _():
        for head in range(groups):
            greet((later, head))

    @pl.when(kv == 0)
    def _():
        for head in range(groups):
            greet((earlier, head))

    lane = lax.broadcasted_iota(jnp.int32, (rows, LANES), 1)
    low = lane < HEAD_DIM
    first_half = lane % HEAD_DIM < HALF
    which = lax.broadcasted_iota(jnp.int32, (1, LANES), 1) % HALF
    inverse = jnp.zeros((1, LANES), F32)
    for i in range(HALF):
        inverse = jnp.where(which == i, 10000.0 ** (-2.0 * i / HEAD_DIM), inverse)
    positions = me * rows + lax.broadcasted_iota(jnp.int32, (rows, LANES), 0)
    angle = positions.astype(F32) * inverse
    cosine = jnp.cos(angle)
    sine = jnp.sin(angle)
    sine = jnp.where(first_half, -sine, sine)

    def rotated(part):
        swapped = jnp.where(
            first_half, pltpu.roll(part, LANES - HALF, 1), pltpu.roll(part, HALF, 1)
        )
        return part * cosine + swapped * sine

    loads[0].wait()
    loads[1].wait()
    inputs = frames_ref[...].astype(F32)
    halo_send[0] = inputs[:HALO].astype(BF16)
    halo_send[1] = inputs[rows - HALO :].astype(BF16)
    normed = layer_norm(inputs, attn_gain_ref[...]).astype(BF16)
    loads[2].wait()
    keys = matmul(normed, w_key[...])
    loads[3].wait()
    values = matmul(normed, w_value[...])
    loads[4].wait()
    queries = matmul(normed, w_query[...])
    to_log2 = 0.125 / math.log(2.0)
    for pair in range(groups // 2):
        at = slice(pair * LANES, (pair + 1) * LANES)
        key = rotated(keys[:, at])
        query = rotated(queries[:, at]) * to_log2
        value = values[:, at]
        key_value = jnp.where(low, key, pltpu.roll(value, HEAD_DIM, 1))
        head_send[2 * pair] = jnp.concatenate(
            [key_value, jnp.where(low, query, 0.0)], axis=0
        ).astype(BF16)
        key_value = jnp.where(low, pltpu.roll(key, HEAD_DIM, 1), value)
        head_send[2 * pair + 1] = jnp.concatenate(
            [key_value, jnp.where(low, pltpu.roll(query, HEAD_DIM, 1), 0.0)], axis=0
        ).astype(BF16)

    pl.semaphore_wait(barrier, groups - 1 + 2 * (side - 1) + 2)

    head_copies = [
        pltpu.make_async_remote_copy(
            src_ref=head_send.at[(kv + d) % groups],
            dst_ref=head_recv.at[kv],
            send_sem=head_ssem.at[d],
            recv_sem=head_rsem.at[d],
            device_id=kv_peer(d),
            device_id_type=MESH,
        )
        for d in range(1, groups)
    ]
    for copy in head_copies:
        copy.start()
    halo_copies = [
        pltpu.make_async_remote_copy(
            src_ref=halo_send.at[i],
            dst_ref=halo_recv.at[i],
            send_sem=halo_ssem.at[i],
            recv_sem=halo_rsem.at[i],
            device_id=target,
            device_id_type=MESH,
        )
        for i, target in enumerate((preceding, following))
    ]
    for copy in halo_copies:
        copy.start()
    for load in loads[5:]:
        load.start()
    head_recv[kv] = head_send[kv]
    kv_wide[:, LANES:] = jnp.ones((kv_wide.shape[0], LANES), BF16)
    for copy in head_copies:
        copy.wait_recv()
    pieces = [head_recv[head].astype(F32) for head in range(groups)]
    own_block = jnp.concatenate([piece[:rows] for piece in pieces], axis=0).astype(BF16)
    kv_all[0] = own_block

    def kv_copy(d):
        return pltpu.make_async_remote_copy(
            src_ref=kv_all.at[0],
            dst_ref=kv_all.at[d],
            send_sem=kv_ssem.at[d],
            recv_sem=kv_rsem.at[d],
            device_id=key_peer(d),
            device_id_type=MESH,
        )

    def q_copy(d):
        return pltpu.make_async_remote_copy(
            src_ref=q_all.at[0],
            dst_ref=q_all.at[d],
            send_sem=q_ssem.at[d],
            recv_sem=q_rsem.at[d],
            device_id=query_peer(d),
            device_id_type=MESH,
        )

    for d in near:
        kv_copy(d).start()
    own_queries = jnp.concatenate([piece[rows:] for piece in pieces], axis=0)
    q_all[0] = (
        own_queries[:half_block] + pltpu.roll(own_queries[half_block:], HEAD_DIM, 1)
    ).astype(BF16)
    for d in near:
        q_copy(d).start()

    kv_wide[0:block, :LANES] = own_block
    for d in near:
        kv_copy(d).wait_recv()
        kv_wide[d * block : (d + 1) * block, :LANES] = kv_all[d]

    half_lane = lax.broadcasted_iota(jnp.int32, (half_block, LANES), 1)
    block_lane = lax.broadcasted_iota(jnp.int32, (block, LANES), 1)
    step_lane = lax.broadcasted_iota(jnp.int32, (2 * block, LANES), 1)

    def unfolded(d):
        packed = q_all[d].astype(F32)
        return [
            jnp.where(half_lane < HEAD_DIM, packed, 0.0),
            jnp.where(half_lane < HEAD_DIM, pltpu.roll(packed, HEAD_DIM, 1), 0.0),
        ]

    def attend(first, second):
        query = jnp.concatenate(unfolded(first) + unfolded(second), axis=0).astype(BF16)
        score = lax.dot_general(
            query, kv_wide[:, :LANES], (((1,), (1,)), ((), ())), preferred_element_type=F32
        )
        top = jnp.max(score, axis=1, keepdims=True)
        weight = jnp.exp2(score - top).astype(BF16)
        mixed = matmul(weight, kv_wide[...])
        total = mixed[:, LANES:]
        level = top + jnp.log2(total)
        high = level.astype(BF16).astype(F32)
        part = jnp.where(
            step_lane >= HEAD_DIM,
            mixed[:, :LANES] / total,
            jnp.where(step_lane < HALF, high, level - high),
        ).astype(BF16)
        part_send[first] = part[:block]
        part_send[second] = part[block:]

    def part_copy(d):
        return pltpu.make_async_remote_copy(
            src_ref=part_send.at[d],
            dst_ref=part_recv.at[d],
            send_sem=part_ssem.at[d],
            recv_sem=part_rsem.at[d],
            device_id=query_peer(side - d),
            device_id_type=MESH,
        )

    order = [0] + near[2:] + near[:2]

    def in_order(step):
        return sum((step == i).astype(jnp.int32) * d for i, d in enumerate(order))

    @pl.loop(0, side // 2)
    def _(step):
        first = in_order(2 * step)
        second = in_order(2 * step + 1)

        @pl.when(step > 0)
        def _():
            q_copy(first).wait_recv()

        q_copy(second).wait_recv()
        attend(first, second)

        @pl.when(step > 0)
        def _():
            part_copy(first).start()

        part_copy(second).start()

    part_recv[0] = part_send[0]
    for d in range(1, side):
        part_copy(d).wait_recv()

    parts = part_recv[...].reshape(side * block, LANES)
    pick = lax.broadcasted_iota(jnp.int32, (LANES, LANES), 0)
    pick = jnp.where((pick == 0) | (pick == HALF), 1.0, 0.0).astype(BF16)
    levels = matmul(parts, pick).reshape(side, block, LANES)
    parts = parts.astype(F32).reshape(side, block, LANES)
    fades = jnp.exp2(levels - jnp.max(levels, axis=0, keepdims=True))
    merged = jnp.sum(fades * parts, axis=0) / jnp.sum(fades, axis=0)

    edge_send[0] = folded(merged[: 2 * HALO])
    edge_send[1] = folded(merged[block - 2 * HALO :])
    framed = jnp.concatenate(
        [jnp.zeros((HALO, LANES), F32), merged, jnp.zeros((WINDOW - rows - HALO, LANES), F32)],
        axis=0,
    )
    for part in range(groups):
        ctx_send[part] = folded(framed[part * rows : part * rows + WINDOW])

    def edge_copy(i, head):
        return pltpu.make_async_remote_copy(
            src_ref=edge_send.at[i],
            dst_ref=edge_recv.at[head],
            send_sem=edge_ssem.at[i],
            recv_sem=edge_rsem.at[head],
            device_id=((earlier, groups - 1), (later, 0))[i],
            device_id_type=MESH,
        )

    for i in range(2):
        edge_copy(i, kv).start()
    ctx_copies = [
        pltpu.make_async_remote_copy(
            src_ref=ctx_send.at[(kv + d) % groups],
            dst_ref=ctx_recv.at[kv],
            send_sem=ctx_ssem.at[d],
            recv_sem=ctx_rsem.at[d],
            device_id=kv_peer(d),
            device_id_type=MESH,
        )
        for d in range(1, groups)
    ]
    for copy in ctx_copies:
        copy.start()
    ctx_recv[kv] = ctx_send[kv]
    for load in loads[5:]:
        load.wait()
    for copy in halo_copies:
        copy.wait_recv()
    extent = rows + 2 * HALO
    nearby = jnp.concatenate([halo_recv[1].astype(F32), inputs, halo_recv[0].astype(F32)], axis=0)
    for copy in ctx_copies:
        copy.wait_recv()
    context[...] = all_heads(ctx_recv)[:extent]

    @pl.when(kv == 0)
    def _():
        for head in range(groups):
            edge_copy(1, head).wait_recv()
        context[:HALO] = all_heads(edge_recv)[HALO:]

    @pl.when(kv == groups - 1)
    def _():
        for head in range(groups):
            edge_copy(0, head).wait_recv()
        context[extent - HALO :] = all_heads(edge_recv)[:HALO]

    attended = matmul(context[...].astype(BF16), w_out[...]).astype(BF16).astype(F32)
    attended_ref[...] = attended[HALO : HALO + rows].astype(BF16)
    stores = [
        pltpu.make_async_copy(attended_ref, attended_hbm, store_sem.at[0]),
        pltpu.make_async_copy(layer_ref, layer_hbm, store_sem.at[1]),
    ]
    stores[0].start()
    mid = nearby + attended
    conv_in = layer_norm(mid, conv_gain_ref[...]).astype(BF16)
    expanded = matmul(conv_in, w_expand[...])
    gate = expanded[:, width:]
    glu = (expanded[:, :width] / (1.0 + jnp.exp(-gate))).astype(BF16).astype(F32)
    times = me * rows - HALO + lax.broadcasted_iota(jnp.int32, (extent, width), 0)
    padded[...] = jnp.where((times >= 0) & (times < devices * rows), glu, 0.0)

    depth = jnp.zeros((rows, width), F32)
    count = taps_ref.shape[0]
    for turn in range(8):
        shifted = None
        for tap in range(turn - 1, count, 8):
            if tap < 0:
                continue
            term = taps_ref[tap : tap + 1] * padded[tap + 1 - turn : tap + 9 - turn + rows]
            shifted = term if shifted is None else shifted + term
        depth = depth + shifted[turn : turn + rows]
    batch = depth * scale_ref[...] + shift_ref[...]
    act = (batch / (1.0 + jnp.exp(-batch))).astype(BF16)
    layer_ref[...] = (mid[HALO : HALO + rows] + matmul(act, w_project[...])).astype(BF16)
    stores[1].start()

    for copy in head_copies + halo_copies + ctx_copies:
        copy.wait_send()
    for d in range(1, side):
        kv_copy(d).wait_send()
        q_copy(d).wait_send()
        part_copy(d).wait_send()
    for i in range(2):
        edge_copy(i, kv).wait_send()
    for store in stores:
        store.wait()


def copy_kernel(attended_in, layer_in, attended_out, layer_out, sem):
    copies = [
        pltpu.make_async_copy(attended_in, attended_out, sem.at[0]),
        pltpu.make_async_copy(layer_in, layer_out, sem.at[1]),
    ]
    for copy in copies:
        copy.start()
    for copy in copies:
        copy.wait()


def on_device(
    frames,
    attn_gain,
    w_query,
    w_key,
    w_value,
    w_out,
    conv_gain,
    w_expand,
    kernel,
    bn_scale,
    bn_shift,
    w_project,
):
    rows, width = frames.shape
    groups = lax.axis_size("kv")
    side = math.isqrt(lax.axis_size("tm"))
    block = rows * groups
    anywhere = pl.BlockSpec(memory_space=pl.ANY)
    dma = pltpu.SemaphoreType.DMA
    results = pl.pallas_call(
        functools.partial(layer_kernel, side),
        out_shape=(
            jax.ShapeDtypeStruct((rows, width), BF16),
            jax.ShapeDtypeStruct((rows, width), BF16),
        ),
        in_specs=[anywhere] * 12,
        out_specs=(anywhere, anywhere),
        scratch_shapes=[
            pltpu.VMEM((rows, width), BF16),
            pltpu.VMEM((rows, width), BF16),
            pltpu.VMEM((rows, width), BF16),
            pltpu.VMEM((1, width), F32),
            pltpu.VMEM((1, width), F32),
            pltpu.VMEM(kernel.shape, F32),
            pltpu.VMEM((1, width), F32),
            pltpu.VMEM((1, width), F32),
            pltpu.VMEM((width, width), BF16),
            pltpu.VMEM((width, width), BF16),
            pltpu.VMEM((width, width), BF16),
            pltpu.VMEM((width, width), BF16),
            pltpu.VMEM((width, 2 * width), BF16),
            pltpu.VMEM((width, width), BF16),
            pltpu.VMEM((groups, 2 * rows, LANES), BF16),
            pltpu.VMEM((groups, 2 * rows, LANES), BF16),
            pltpu.VMEM((side, block, LANES), BF16),
            pltpu.VMEM((side * block, 2 * LANES), BF16),
            pltpu.VMEM((side, block // 2, LANES), BF16),
            pltpu.VMEM((side, block, LANES), BF16),
            pltpu.VMEM((side, block, LANES), BF16),
            pltpu.VMEM((groups, WINDOW // 2, LANES), BF16),
            pltpu.VMEM((groups, WINDOW // 2, LANES), BF16),
            pltpu.VMEM((2, HALO, LANES), BF16),
            pltpu.VMEM((groups, HALO, LANES), BF16),
            pltpu.VMEM((rows + 2 * HALO, width), F32),
            pltpu.VMEM((2, HALO, width), BF16),
            pltpu.VMEM((2, HALO, width), BF16),
            pltpu.VMEM((rows + 2 * HALO, width), F32),
            dma((12,)),
            dma((2,)),
            dma((groups,)),
            dma((groups,)),
            dma((side,)),
            dma((side,)),
            dma((side,)),
            dma((side,)),
            dma((side,)),
            dma((side,)),
            dma((groups,)),
            dma((groups,)),
            dma((2,)),
            dma((groups,)),
            dma((2,)),
            dma((2,)),
        ],
        compiler_params=pltpu.CompilerParams(
            collective_id=0, has_side_effects=True, vmem_limit_bytes=60 * 1024 * 1024
        ),
    )(
        frames,
        attn_gain.reshape(1, width),
        conv_gain.reshape(1, width),
        kernel,
        bn_scale.reshape(1, width),
        bn_shift.reshape(1, width),
        w_query,
        w_key,
        w_value,
        w_out,
        w_expand,
        w_project,
    )
    return pl.pallas_call(
        copy_kernel,
        out_shape=tuple(jax.ShapeDtypeStruct(r.shape, r.dtype) for r in results),
        in_specs=[anywhere] * 2,
        out_specs=(anywhere, anywhere),
        scratch_shapes=[dma((2,))],
        compiler_params=pltpu.CompilerParams(vmem_limit_bytes=60 * 1024 * 1024),
    )(*results)


def solution(mesh):
    rows = P(("tm", "kv"), None)
    return jax.shard_map(
        on_device,
        mesh=mesh,
        in_specs=(rows,) + (P(),) * 11,
        out_specs=(rows, rows),
        check_vma=False,
    )
```

time: 264 us -> 49.7 us (0.19); the launches traced: 261 us -> 49.6 us
  waiting for transfers between devices: 145 us -> 0 us
  blocking collectives: 49.9 us -> 0 us
  Pallas kernels: 0 us -> 48.9 us
  local copies, waits for them, and re-layouts: 22.9 us -> 0 us
  between operations: 14.1 us -> 0.64 us
  matrix products: 13.3 us -> 0 us
  other arithmetic: 10.3 us -> 0 us
  starting transfers between devices: 4.91 us -> 0 us
    all_gather x3 -> x0, waiting for transfers between devices: 142 us -> none  [the longest x1 80.7 us: on_device(): lax.all_gather(k_local, 'tm', axis=0, tiled=True)]
    all_gather x3 -> x0, blocking collectives: 49.9 us -> none  [the longest x2 30.4 us: merged_2(): everything = jax.tree.map(lambda part: lax.all_gather(part, axis), x)]
    pallas_call x0 -> x2, Pallas kernels: none -> 48.9 us  [the longest x1 46.3 us: on_device(): pl.pallas_call(functools.partial(layer_kernel, side), out_shape=(jax.Shap...]
    dot_general x12 -> x0, matrix products: 13.3 us -> none  [the longest x3 3.18 us: absorb(): jnp.einsum('qhd,khd->qhk', queries, key_block, preferred_element_type=jnp...]
    slice x11 -> x0, local copies, waits for them, and re-layouts: 10.8 us -> none  [the longest x4 5.99 us: absorb(): value_block = values[begin:begin + 512]]
    dynamic_slice x15 -> x0, local copies, waits for them, and re-layouts: 8.71 us -> none  [the longest x14 8.63 us: turn(): return combine(so_far, jax.tree.map(lambda part: part[k], everything))]
    reduce_sum x6 -> x0, other arithmetic: 7.96 us -> none  [the longest x2 5.81 us: absorb(): total = total * fade + jnp.sum(weight, axis=-1)]
    ppermute x2 -> x0, starting transfers between devices: 4.79 us -> none  [the longest x1 2.87 us: extended(): lax.ppermute(tail, axis, [(i, (i + 1) % count) for i in range(ends)])]
  transfers between devices with their start and end apart: 5 -> 0, of which waited for: 3 -> 0; matrix products, arithmetic and copies ran while one was open for 5% -> 0% of each run, Pallas kernels for 0% -> 0%
where the time goes in v1:
time: 49.7 us; the launch traced here: 49.6 us
  Pallas kernels  48.9 us (98%)
  between operations  0.64 us (1%)
    pallas_call x1, Pallas kernels, on_device(): pl.pallas_call(functools.partial(layer_kernel, side), out_shape=(jax.Shap...  46.3 us
    pallas_call x1, Pallas kernels, on_device(): pl.pallas_call(copy_kernel, out_shape=tuple((jax.ShapeDtypeStruct(r.shape...  2.61 us

profile of v1, /device:TPU:1, one launch (start us, length us, event | category | flops | bytes accessed | tf_op | source)
XLA Modules:
  0.0 49.6 jit_solution(6942949488651886980)
XLA Ops:
  0.6 46.3 %shard_map.131 = (bf16[24,512]{1,0:T(8,128)(2,1)}, bf16[24,512]{1,0:T(8,128)(2,1)}) custom-call(bf16[24,512]{1,0:T(8,128)(2,1)} %frames_hbm.1, f32[1,512]{1,0:T(1,128)} %bitcast.4, f32[1,512]{1,0:T(1,128)} %bitcast.5, f32[31,512]{1,0:T(8,128)} %taps_hbm.1, f32[1,512]{1,0:T(1,128)} %bitcast.6, f32[1,512]{1,0:T(1,128)} %bitcast.7, ...), custom_call_target="tpu_custom_call" | custom-call | tf_op jit(solution)/shard_map/pallas_call | solution.py:511
  46.9 2.6 %shard_map.132 = (bf16[24,512]{1,0:T(8,128)(2,1)}, bf16[24,512]{1,0:T(8,128)(2,1)}) custom-call(bf16[24,512]{1,0:T(8,128)(2,1)} %get-tuple-element.4.attended_in, bf16[24,512]{1,0:T(8,128)(2,1)} %get-tuple-element.5.layer_in), custom_call_target="tpu_custom_call" | custom-call | tf_op jit(solution)/shard_map/pallas_call | solution.py:583

commit v2 on v1

--- a/solution.py
+++ b/solution.py
@@ -13,6 +13,7 @@
 LANES = 128
 HALO = 16
 WINDOW = 64
+CHUNK = 32
 MESH = pl.DeviceIdType.MESH
 BF16 = jnp.bfloat16
 F32 = jnp.float32
@@ -50,27 +51,19 @@
 def layer_kernel(
     side,
     frames_hbm,
-    attn_gain_hbm,
-    conv_gain_hbm,
+    gains_hbm,
     taps_hbm,
-    scale_hbm,
-    shift_hbm,
     w_query_hbm,
     w_key_hbm,
     w_value_hbm,
     w_out_hbm,
     w_expand_hbm,
     w_project_hbm,
-    attended_hbm,
-    layer_hbm,
     attended_ref,
     layer_ref,
     frames_ref,
-    attn_gain_ref,
-    conv_gain_ref,
+    gains_ref,
     taps_ref,
-    scale_ref,
-    shift_ref,
     w_query,
     w_key,
     w_value,
@@ -81,7 +74,11 @@
     head_recv,
     kv_all,
     kv_wide,
+    key_rows,
     q_all,
+    scores,
+    weights,
+    tops,
     part_send,
     part_recv,
     ctx_send,
@@ -93,7 +90,6 @@
     halo_recv,
     padded,
     load_sem,
-    store_sem,
     head_ssem,
     head_rsem,
     kv_ssem,
@@ -151,16 +147,13 @@
         for i, (source, target) in enumerate(
             (
                 (frames_hbm, frames_ref),
-                (attn_gain_hbm, attn_gain_ref),
+                (gains_hbm, gains_ref),
                 (w_key_hbm, w_key),
                 (w_value_hbm, w_value),
                 (w_query_hbm, w_query),
                 (w_out_hbm, w_out),
-                (conv_gain_hbm, conv_gain_ref),
                 (w_expand_hbm, w_expand),
                 (taps_hbm, taps_ref),
-                (scale_hbm, scale_ref),
-                (shift_hbm, shift_ref),
                 (w_project_hbm, w_project),
             )
         )
@@ -209,7 +202,7 @@
     inputs = frames_ref[...].astype(F32)
     halo_send[0] = inputs[:HALO].astype(BF16)
     halo_send[1] = inputs[rows - HALO :].astype(BF16)
-    normed = layer_norm(inputs, attn_gain_ref[...]).astype(BF16)
+    normed = layer_norm(inputs, gains_ref[0:1]).astype(BF16)
     loads[2].wait()
     keys = matmul(normed, w_key[...])
     loads[3].wait()
@@ -269,39 +262,62 @@
     own_block = jnp.concatenate([piece[:rows] for piece in pieces], axis=0).astype(BF16)
     kv_all[0] = own_block
 
-    def kv_copy(d):
-        return pltpu.make_async_remote_copy(
-            src_ref=kv_all.at[0],
-            dst_ref=kv_all.at[d],
-            send_sem=kv_ssem.at[d],
-            recv_sem=kv_rsem.at[d],
-            device_id=key_peer(d),
-            device_id_type=MESH,
-        )
-
-    def q_copy(d):
-        return pltpu.make_async_remote_copy(
-            src_ref=q_all.at[0],
-            dst_ref=q_all.at[d],
-            send_sem=q_ssem.at[d],
-            recv_sem=q_rsem.at[d],
-            device_id=query_peer(d),
-            device_id_type=MESH,
-        )
-
-    for d in near:
-        kv_copy(d).start()
+    def line_copies(ref, ssem, rsem, peer):
+        half = ref.shape[1] // 2
+        lower, upper = pl.ds(0, half), pl.ds(half, half)
+
+        def copy(source, target, place, sem):
+            return pltpu.make_async_remote_copy(
+                src_ref=source,
+                dst_ref=target,
+                send_sem=ssem.at[sem],
+                recv_sem=rsem.at[sem],
+                device_id=peer(place),
+                device_id_type=MESH,
+            )
+
+        if side < 8:
+            return {d: copy(ref.at[0], ref.at[d], d, d) for d in near}, {}
+        direct = {d: copy(ref.at[0], ref.at[d], d, d) for d in near[:4]}
+        relayed = {
+            2: {
+                3: copy(ref.at[2], ref.at[3], 1, 3),
+                4: copy(ref.at[2, lower], ref.at[4, lower], 2, 4),
+            },
+            6: {
+                5: copy(ref.at[6], ref.at[5], 7, 5),
+                0: copy(ref.at[6, upper], ref.at[4, upper], 6, 0),
+            },
+        }
+        return direct, relayed
+
+    kv_direct, kv_relayed = line_copies(kv_all, kv_ssem, kv_rsem, key_peer)
+    q_direct, q_relayed = line_copies(q_all, q_ssem, q_rsem, query_peer)
+    lines = ((kv_direct, kv_relayed), (q_direct, q_relayed))
+    for copy in kv_direct.values():
+        copy.start()
     own_queries = jnp.concatenate([piece[rows:] for piece in pieces], axis=0)
     q_all[0] = (
         own_queries[:half_block] + pltpu.roll(own_queries[half_block:], HEAD_DIM, 1)
     ).astype(BF16)
-    for d in near:
-        q_copy(d).start()
-
-    kv_wide[0:block, :LANES] = own_block
-    for d in near:
-        kv_copy(d).wait_recv()
-        kv_wide[d * block : (d + 1) * block, :LANES] = kv_all[d]
+    for copy in q_direct.values():
+        copy.start()
+    for direct, relayed in lines:
+        for d, onward in relayed.items():
+            direct[d].wait_recv()
+            for copy in onward.values():
+                copy.start()
+    for direct, relayed in lines:
+        for d, copy in direct.items():
+            if d not in relayed:
+                copy.wait_recv()
+        for onward in relayed.values():
+            for copy in onward.values():
+                copy.wait_recv()
+    kv_wide[:, :LANES] = kv_all[...].reshape(side * block, LANES)
+    for d in range(0, side, 2):
+        both = kv_all[d : d + 2].astype(F32).reshape(2 * block, LANES)
+        key_rows[:, d * block : (d + 2) * block] = both.T.astype(BF16)
 
     half_lane = lax.broadcasted_iota(jnp.int32, (half_block, LANES), 1)
     block_lane = lax.broadcasted_iota(jnp.int32, (block, LANES), 1)
@@ -316,14 +332,16 @@
 
     def attend(first, second):
         query = jnp.concatenate(unfolded(first) + unfolded(second), axis=0).astype(BF16)
-        score = lax.dot_general(
-            query, kv_wide[:, :LANES], (((1,), (1,)), ((), ())), preferred_element_type=F32
-        )
-        top = jnp.max(score, axis=1, keepdims=True)
-        weight = jnp.exp2(score - top).astype(BF16)
-        mixed = matmul(weight, kv_wide[...])
+        scores[...] = matmul(query, key_rows[...])
+        for begin in range(0, 2 * block, CHUNK):
+            at = slice(begin, begin + CHUNK)
+            score = scores[at]
+            top = jnp.max(score, axis=1, keepdims=True)
+            weights[at] = jnp.exp2(score - top).astype(BF16)
+            tops[at] = jnp.broadcast_to(top, (CHUNK, LANES))
+        mixed = matmul(weights[...], kv_wide[...])
         total = mixed[:, LANES:]
-        level = top + jnp.log2(total)
+        level = tops[...] + jnp.log2(total)
         high = level.astype(BF16).astype(F32)
         part = jnp.where(
             step_lane >= HEAD_DIM,
@@ -343,7 +361,7 @@
             device_id_type=MESH,
         )
 
-    order = [0] + near[2:] + near[:2]
+    order = [0] + near[::-1]
 
     def in_order(step):
         return sum((step == i).astype(jnp.int32) * d for i, d in enumerate(order))
@@ -353,11 +371,6 @@
         first = in_order(2 * step)
         second = in_order(2 * step + 1)
 
-        @pl.when(step > 0)
-        def _():
-            q_copy(first).wait_recv()
-
-        q_copy(second).wait_recv()
         attend(first, second)
 
         @pl.when(step > 0)
@@ -437,13 +450,8 @@
 
     attended = matmul(context[...].astype(BF16), w_out[...]).astype(BF16).astype(F32)
     attended_ref[...] = attended[HALO : HALO + rows].astype(BF16)
-    stores = [
-        pltpu.make_async_copy(attended_ref, attended_hbm, store_sem.at[0]),
-        pltpu.make_async_copy(layer_ref, layer_hbm, store_sem.at[1]),
-    ]
-    stores[0].start()
     mid = nearby + attended
-    conv_in = layer_norm(mid, conv_gain_ref[...]).astype(BF16)
+    conv_in = layer_norm(mid, gains_ref[1:2]).astype(BF16)
     expanded = matmul(conv_in, w_expand[...])
     gate = expanded[:, width:]
     glu = (expanded[:, :width] / (1.0 + jnp.exp(-gate))).astype(BF16).astype(F32)
@@ -460,21 +468,22 @@
             term = taps_ref[tap : tap + 1] * padded[tap + 1 - turn : tap + 9 - turn + rows]
             shifted = term if shifted is None else shifted + term
         depth = depth + shifted[turn : turn + rows]
-    batch = depth * scale_ref[...] + shift_ref[...]
+    batch = depth * gains_ref[2:3] + gains_ref[3:4]
     act = (batch / (1.0 + jnp.exp(-batch))).astype(BF16)
     layer_ref[...] = (mid[HALO : HALO + rows] + matmul(act, w_project[...])).astype(BF16)
-    stores[1].start()
 
     for copy in head_copies + halo_copies + ctx_copies:
         copy.wait_send()
     for d in range(1, side):
-        kv_copy(d).wait_send()
-        q_copy(d).wait_send()
         part_copy(d).wait_send()
+    for direct, relayed in lines:
+        for copy in direct.values():
+            copy.wait_send()
+        for onward in relayed.values():
+            for copy in onward.values():
+                copy.wait_send()
     for i in range(2):
         edge_copy(i, kv).wait_send()
-    for store in stores:
-        store.wait()
 
 
 def copy_kernel(attended_in, layer_in, attended_out, layer_out, sem):
@@ -506,6 +515,7 @@
     groups = lax.axis_size("kv")
     side = math.isqrt(lax.axis_size("tm"))
     block = rows * groups
+    vmem = pl.BlockSpec(memory_space=pltpu.VMEM)
     anywhere = pl.BlockSpec(memory_space=pl.ANY)
     dma = pltpu.SemaphoreType.DMA
     results = pl.pallas_call(
@@ -514,17 +524,12 @@
             jax.ShapeDtypeStruct((rows, width), BF16),
             jax.ShapeDtypeStruct((rows, width), BF16),
         ),
-        in_specs=[anywhere] * 12,
-        out_specs=(anywhere, anywhere),
+        in_specs=[anywhere] * 9,
+        out_specs=(vmem, vmem),
         scratch_shapes=[
             pltpu.VMEM((rows, width), BF16),
-            pltpu.VMEM((rows, width), BF16),
-            pltpu.VMEM((rows, width), BF16),
-            pltpu.VMEM((1, width), F32),
-            pltpu.VMEM((1, width), F32),
+            pltpu.VMEM((4, width), F32),
             pltpu.VMEM(kernel.shape, F32),
-            pltpu.VMEM((1, width), F32),
-            pltpu.VMEM((1, width), F32),
             pltpu.VMEM((width, width), BF16),
             pltpu.VMEM((width, width), BF16),
             pltpu.VMEM((width, width), BF16),
@@ -535,7 +540,11 @@
             pltpu.VMEM((groups, 2 * rows, LANES), BF16),
             pltpu.VMEM((side, block, LANES), BF16),
             pltpu.VMEM((side * block, 2 * LANES), BF16),
+            pltpu.VMEM((LANES, side * block), BF16),
             pltpu.VMEM((side, block // 2, LANES), BF16),
+            pltpu.VMEM((2 * block, side * block), F32),
+            pltpu.VMEM((2 * block, side * block), BF16),
+            pltpu.VMEM((2 * block, LANES), F32),
             pltpu.VMEM((side, block, LANES), BF16),
             pltpu.VMEM((side, block, LANES), BF16),
             pltpu.VMEM((groups, WINDOW // 2, LANES), BF16),
@@ -546,8 +555,7 @@
             pltpu.VMEM((2, HALO, width), BF16),
             pltpu.VMEM((2, HALO, width), BF16),
             pltpu.VMEM((rows + 2 * HALO, width), F32),
-            dma((12,)),
-            dma((2,)),
+            dma((9,)),
             dma((groups,)),
             dma((groups,)),
             dma((side,)),
@@ -564,15 +572,12 @@
             dma((2,)),
         ],
         compiler_params=pltpu.CompilerParams(
-            collective_id=0, has_side_effects=True, vmem_limit_bytes=60 * 1024 * 1024
+            collective_id=0, has_side_effects=True, vmem_limit_bytes=55160 * 1024
         ),
     )(
         frames,
-        attn_gain.reshape(1, width),
-        conv_gain.reshape(1, width),
+        jnp.stack([attn_gain, conv_gain, bn_scale, bn_shift]),
         kernel,
-        bn_scale.reshape(1, width),
-        bn_shift.reshape(1, width),
         w_query,
         w_key,
         w_value,
@@ -583,10 +588,10 @@
     return pl.pallas_call(
         copy_kernel,
         out_shape=tuple(jax.ShapeDtypeStruct(r.shape, r.dtype) for r in results),
-        in_specs=[anywhere] * 2,
+        in_specs=[vmem] * 2,
         out_specs=(anywhere, anywhere),
         scratch_shapes=[dma((2,))],
-        compiler_params=pltpu.CompilerParams(vmem_limit_bytes=60 * 1024 * 1024),
+        compiler_params=pltpu.CompilerParams(vmem_limit_bytes=4 * 1024 * 1024),
     )(*results)
 
 

time: 49.7 us -> 48 us (0.966)
  Pallas kernels: 48.9 us -> 45.7 us
  other arithmetic: 0 us -> 0.69 us
  local copies, waits for them, and re-layouts: 0 us -> 0.69 us
    pallas_call x1, Pallas kernels: 2.61 us -> 0.64 us  [on_device(): pl.pallas_call(copy_kernel, out_shape=tuple((jax.ShapeDtypeStruct(r.shape...]
    pallas_call x1, Pallas kernels: 46.3 us -> 45.1 us  [on_device(): pl.pallas_call(functools.partial(layer_kernel, side), out_shape=(jax.Shap...]
    another operation x0 -> x1, other arithmetic: none -> 0.69 us  [on_device(): jnp.stack([attn_gain, conv_gain, bn_scale, bn_shift])]
    unnamed x0 -> x6, local copies, waits for them, and re-layouts: none -> 0.69 us
where the time goes in v2:
time: 48 us; the launch traced here: 47.8 us
  Pallas kernels  45.7 us (95%)
  local copies, waits for them, and re-layouts  0.69 us (1%)
  other arithmetic  0.69 us (1%)
  between operations  0.67 us (1%)
    pallas_call x1, Pallas kernels, on_device(): pl.pallas_call(functools.partial(layer_kernel, side), out_shape=(jax.Shap...  45.1 us

profile of v2, /device:TPU:1, one launch (start us, length us, event | category | flops | bytes accessed | tf_op | source)
XLA Modules:
  0.0 47.8 jit_solution(7825682011226098499)
XLA Ops:
  0.6 0.0 copy-start.2
  0.6 0.0 copy-start.1
  0.7 0.0 copy-start
  0.7 0.7 %copy-done.2 = f32[512]{0:T(512)S(1)} copy-done((f32[512]{0:T(512)S(1)}, f32[512]{0:T(512)}, u32[]{:S(2)}) %copy-start.2) | copy-done | bytes 2072
  1.3 0.0 copy-done.1
  1.3 0.0 copy-done
  1.3 0.7 %pad_maximum_fusion.gains_hbm = f32[4,512]{1,0:T(4,128)S(1)} fusion(f32[1,512]{1,0:T(1,128)S(1)} %bitcast.4, f32[1,512]{1,0:T(1,128)S(1)} %bitcast.5, f32[1,512]{1,0:T(1,128)S(1)} %bitcast.6, f32[1,512]{1,0:T(1,128)} %bitcast.7), kind=kLoop, calls=%fused_computation | loop fusion | flops 6144 | bytes 16384 | tf_op jit(solution)/shard_map/stack | solution.py:579
  2.0 45.1 %shard_map.131 = (bf16[24,512]{1,0:T(8,128)(2,1)S(1)}, bf16[24,512]{1,0:T(8,128)(2,1)S(1)}) custom-call(bf16[24,512]{1,0:T(8,128)(2,1)} %frames_hbm.1, f32[4,512]{1,0:T(4,128)S(1)} %pad_maximum_fusion.gains_hbm, f32[31,512]{1,0:T(8,128)} %taps_hbm.1, bf16[512,512]{1,0:T(8,128)(2,1)} %w_query_hbm.1, bf16[512,512]{1,0:T(8,128)(2,1)} %w_key_hbm.1, ...), custom_call_target="tpu_custom_call" | custom-call | tf_op jit(solution)/shard_map/pallas_call | solution.py:521
  47.1 0.6 %shard_map.132 = (bf16[24,512]{1,0:T(8,128)(2,1)}, bf16[24,512]{1,0:T(8,128)(2,1)}) custom-call(bf16[24,512]{1,0:T(8,128)(2,1)S(1)} %get-tuple-element.4.attended_in, bf16[24,512]{1,0:T(8,128)(2,1)S(1)} %get-tuple-element.5.layer_in), custom_call_target="tpu_custom_call" | custom-call | tf_op jit(solution)/shard_map/pallas_call | solution.py:588
Async XLA Ops:
  0.6 0.7 %copy-start.2 = (f32[512]{0:T(512)S(1)}, f32[512]{0:T(512)}, u32[]{:S(2)}) copy-start(f32[512]{0:T(512)} %param.18) | copy-start | bytes 6148
  0.6 0.7 %copy-start.1 = (f32[512]{0:T(512)S(1)}, f32[512]{0:T(512)}, u32[]{:S(2)}) copy-start(f32[512]{0:T(512)} %param.21) | copy-start | bytes 6148
  0.7 0.7 %copy-start = (f32[512]{0:T(512)S(1)}, f32[512]{0:T(512)}, u32[]{:S(2)}) copy-start(f32[512]{0:T(512)} %param.22) | copy-start | bytes 6148

commit v3 on v2

--- a/solution.py
+++ b/solution.py
@@ -51,7 +51,10 @@
 def layer_kernel(
     side,
     frames_hbm,
-    gains_hbm,
+    attn_gain_hbm,
+    conv_gain_hbm,
+    scale_hbm,
+    shift_hbm,
     taps_hbm,
     w_query_hbm,
     w_key_hbm,
@@ -59,6 +62,8 @@
     w_out_hbm,
     w_expand_hbm,
     w_project_hbm,
+    attended_hbm,
+    layer_hbm,
     attended_ref,
     layer_ref,
     frames_ref,
@@ -73,12 +78,18 @@
     head_send,
     head_recv,
     kv_all,
-    kv_wide,
-    key_rows,
+    near_wide,
+    far_wide,
+    near_keys,
+    far_keys,
     q_all,
-    scores,
-    weights,
+    near_scores,
+    far_scores,
+    near_weights,
+    far_weights,
     tops,
+    first_mixed,
+    first_tops,
     part_send,
     part_recv,
     ctx_send,
@@ -90,6 +101,7 @@
     halo_recv,
     padded,
     load_sem,
+    store_sem,
     head_ssem,
     head_rsem,
     kv_ssem,
@@ -147,13 +159,16 @@
         for i, (source, target) in enumerate(
             (
                 (frames_hbm, frames_ref),
-                (gains_hbm, gains_ref),
+                (attn_gain_hbm, gains_ref.at[0:1]),
                 (w_key_hbm, w_key),
                 (w_value_hbm, w_value),
                 (w_query_hbm, w_query),
                 (w_out_hbm, w_out),
                 (w_expand_hbm, w_expand),
                 (taps_hbm, taps_ref),
+                (conv_gain_hbm, gains_ref.at[1:2]),
+                (scale_hbm, gains_ref.at[2:3]),
+                (shift_hbm, gains_ref.at[3:4]),
                 (w_project_hbm, w_project),
             )
         )
@@ -255,7 +270,8 @@
     for load in loads[5:]:
         load.start()
     head_recv[kv] = head_send[kv]
-    kv_wide[:, LANES:] = jnp.ones((kv_wide.shape[0], LANES), BF16)
+    for wide in (near_wide, far_wide):
+        wide[:, LANES:] = jnp.ones((wide.shape[0], LANES), BF16)
     for copy in head_copies:
         copy.wait_recv()
     pieces = [head_recv[head].astype(F32) for head in range(groups)]
@@ -307,49 +323,79 @@
             direct[d].wait_recv()
             for copy in onward.values():
                 copy.start()
-    for direct, relayed in lines:
-        for d, copy in direct.items():
-            if d not in relayed:
-                copy.wait_recv()
-        for onward in relayed.values():
-            for copy in onward.values():
-                copy.wait_recv()
-    kv_wide[:, :LANES] = kv_all[...].reshape(side * block, LANES)
-    for d in range(0, side, 2):
-        both = kv_all[d : d + 2].astype(F32).reshape(2 * block, LANES)
-        key_rows[:, d * block : (d + 2) * block] = both.T.astype(BF16)
+    slots = [0] + near
+    near_slots = slots[: near_wide.shape[0] // block]
+    far_slots = slots[len(near_slots) :]
+
+    def wait_for(wanted):
+        for direct, relayed in lines:
+            for d, copy in direct.items():
+                if d in wanted and d not in relayed:
+                    copy.wait_recv()
+            for onward in relayed.values():
+                for d, copy in onward.items():
+                    if (d or 4) in wanted:
+                        copy.wait_recv()
+
+    def lay_out(wanted, wide, keys):
+        for i in range(0, len(wanted), 2):
+            few = wanted[i : i + 2]
+            both = jnp.concatenate([kv_all[d] for d in few], axis=0)
+            at = slice(i * block, (i + len(few)) * block)
+            wide[at, :LANES] = both
+            keys[:, at] = both.astype(F32).T.astype(BF16)
 
     half_lane = lax.broadcasted_iota(jnp.int32, (half_block, LANES), 1)
     block_lane = lax.broadcasted_iota(jnp.int32, (block, LANES), 1)
-    step_lane = lax.broadcasted_iota(jnp.int32, (2 * block, LANES), 1)
 
     def unfolded(d):
         packed = q_all[d].astype(F32)
-        return [
-            jnp.where(half_lane < HEAD_DIM, packed, 0.0),
-            jnp.where(half_lane < HEAD_DIM, pltpu.roll(packed, HEAD_DIM, 1), 0.0),
-        ]
-
-    def attend(first, second):
-        query = jnp.concatenate(unfolded(first) + unfolded(second), axis=0).astype(BF16)
-        scores[...] = matmul(query, key_rows[...])
-        for begin in range(0, 2 * block, CHUNK):
+        return jnp.concatenate(
+            [
+                jnp.where(half_lane < HEAD_DIM, packed, 0.0),
+                jnp.where(half_lane < HEAD_DIM, pltpu.roll(packed, HEAD_DIM, 1), 0.0),
+            ],
+            axis=0,
+        ).astype(BF16)
+
+    def soften(pieces, floor=None):
+        for begin in range(0, block, CHUNK):
             at = slice(begin, begin + CHUNK)
-            score = scores[at]
-            top = jnp.max(score, axis=1, keepdims=True)
-            weights[at] = jnp.exp2(score - top).astype(BF16)
+            score = [scores[at] for scores, _ in pieces]
+            top = functools.reduce(
+                jnp.maximum, [jnp.max(part, axis=1, keepdims=True) for part in score]
+            )
+            if floor is not None:
+                top = jnp.maximum(top, floor[at, :1])
+            for part, (_, weights) in zip(score, pieces):
+                weights[at] = jnp.exp2(part - top).astype(BF16)
             tops[at] = jnp.broadcast_to(top, (CHUNK, LANES))
-        mixed = matmul(weights[...], kv_wide[...])
+
+    def finish(d, mixed):
         total = mixed[:, LANES:]
         level = tops[...] + jnp.log2(total)
         high = level.astype(BF16).astype(F32)
-        part = jnp.where(
-            step_lane >= HEAD_DIM,
+        part_send[d] = jnp.where(
+            block_lane >= HEAD_DIM,
             mixed[:, :LANES] / total,
-            jnp.where(step_lane < HALF, high, level - high),
+            jnp.where(block_lane < HALF, high, level - high),
         ).astype(BF16)
-        part_send[first] = part[:block]
-        part_send[second] = part[block:]
+
+    def chosen(step, order):
+        return sum((step == i).astype(jnp.int32) * d for i, d in enumerate(order))
+
+    wait_for(near_slots)
+    lay_out(near_slots, near_wide, near_keys)
+
+    @pl.loop(0, len(near_slots))
+    def _(step):
+        near_scores[...] = matmul(unfolded(chosen(step, near_slots)), near_keys[...])
+        soften([(near_scores, near_weights)])
+        first_mixed[step] = matmul(near_weights[...], near_wide[...])
+        first_tops[step] = tops[...]
+
+    wait_for(far_slots)
+    lay_out(far_slots, far_wide, far_keys)
 
     def part_copy(d):
         return pltpu.make_async_remote_copy(
@@ -361,23 +407,30 @@
             device_id_type=MESH,
         )
 
-    order = [0] + near[::-1]
-
-    def in_order(step):
-        return sum((step == i).astype(jnp.int32) * d for i, d in enumerate(order))
-
-    @pl.loop(0, side // 2)
+    @pl.loop(0, len(far_slots))
     def _(step):
-        first = in_order(2 * step)
-        second = in_order(2 * step + 1)
-
-        attend(first, second)
-
-        @pl.when(step > 0)
+        d = chosen(step, far_slots[::-1])
+        query = unfolded(d)
+        near_scores[...] = matmul(query, near_keys[...])
+        far_scores[...] = matmul(query, far_keys[...])
+        soften([(near_scores, near_weights), (far_scores, far_weights)])
+        mixed = matmul(near_weights[...], near_wide[...])
+        finish(d, mixed + matmul(far_weights[...], far_wide[...]))
+        part_copy(d).start()
+
+    @pl.loop(0, len(near_slots))
+    def _(step):
+        at = len(near_slots) - 1 - step
+        d = chosen(at, near_slots)
+        far_scores[...] = matmul(unfolded(d), far_keys[...])
+        soften([(far_scores, far_weights)], first_tops.at[at])
+        fade = jnp.exp2(first_tops[at] - tops[...])
+        mixed = first_mixed[at] * jnp.concatenate([fade, fade], axis=1)
+        finish(d, mixed + matmul(far_weights[...], far_wide[...]))
+
+        @pl.when(at > 0)
         def _():
-            part_copy(first).start()
-
-        part_copy(second).start()
+            part_copy(d).start()
 
     part_recv[0] = part_send[0]
     for d in range(1, side):
@@ -450,6 +503,11 @@
 
     attended = matmul(context[...].astype(BF16), w_out[...]).astype(BF16).astype(F32)
     attended_ref[...] = attended[HALO : HALO + rows].astype(BF16)
+    stores = [
+        pltpu.make_async_copy(attended_ref, attended_hbm, store_sem.at[0]),
+        pltpu.make_async_copy(layer_ref, layer_hbm, store_sem.at[1]),
+    ]
+    stores[0].start()
     mid = nearby + attended
     conv_in = layer_norm(mid, gains_ref[1:2]).astype(BF16)
     expanded = matmul(conv_in, w_expand[...])
@@ -471,6 +529,7 @@
     batch = depth * gains_ref[2:3] + gains_ref[3:4]
     act = (batch / (1.0 + jnp.exp(-batch))).astype(BF16)
     layer_ref[...] = (mid[HALO : HALO + rows] + matmul(act, w_project[...])).astype(BF16)
+    stores[1].start()
 
     for copy in head_copies + halo_copies + ctx_copies:
         copy.wait_send()
@@ -484,16 +543,25 @@
                 copy.wait_send()
     for i in range(2):
         edge_copy(i, kv).wait_send()
-
-
-def copy_kernel(attended_in, layer_in, attended_out, layer_out, sem):
-    copies = [
-        pltpu.make_async_copy(attended_in, attended_out, sem.at[0]),
-        pltpu.make_async_copy(layer_in, layer_out, sem.at[1]),
-    ]
-    for copy in copies:
+    for store in stores:
+        store.wait()
+
+
+def copy_kernel(attended_in, layer_in, attended_out, layer_out, attended, layer, sem):
+    def copies(step, *pairs):
+        return [
+            pltpu.make_async_copy(source, target, sem.at[2 * step + i])
+            for i, (source, target) in enumerate(pairs)
+        ]
+
+    inward = copies(0, (attended_in, attended), (layer_in, layer))
+    outward = copies(1, (attended, attended_out), (layer, layer_out))
+    for copy in inward:
         copy.start()
-    for copy in copies:
+    for copy, onward in zip(inward, outward):
+        copy.wait()
+        onward.start()
+    for copy in outward:
         copy.wait()
 
 
@@ -515,7 +583,8 @@
     groups = lax.axis_size("kv")
     side = math.isqrt(lax.axis_size("tm"))
     block = rows * groups
-    vmem = pl.BlockSpec(memory_space=pltpu.VMEM)
+    near_rows = (5 if side == 8 else side // 2) * block
+    far_rows = side * block - near_rows
     anywhere = pl.BlockSpec(memory_space=pl.ANY)
     dma = pltpu.SemaphoreType.DMA
     results = pl.pallas_call(
@@ -524,9 +593,11 @@
             jax.ShapeDtypeStruct((rows, width), BF16),
             jax.ShapeDtypeStruct((rows, width), BF16),
         ),
-        in_specs=[anywhere] * 9,
-        out_specs=(vmem, vmem),
+        in_specs=[anywhere] * 12,
+        out_specs=(anywhere, anywhere),
         scratch_shapes=[
+            pltpu.VMEM((rows, width), BF16),
+            pltpu.VMEM((rows, width), BF16),
             pltpu.VMEM((rows, width), BF16),
             pltpu.VMEM((4, width), F32),
             pltpu.VMEM(kernel.shape, F32),
@@ -539,12 +610,18 @@
             pltpu.VMEM((groups, 2 * rows, LANES), BF16),
             pltpu.VMEM((groups, 2 * rows, LANES), BF16),
             pltpu.VMEM((side, block, LANES), BF16),
-            pltpu.VMEM((side * block, 2 * LANES), BF16),
-            pltpu.VMEM((LANES, side * block), BF16),
+            pltpu.VMEM((near_rows, 2 * LANES), BF16),
+            pltpu.VMEM((far_rows, 2 * LANES), BF16),
+            pltpu.VMEM((LANES, near_rows), BF16),
+            pltpu.VMEM((LANES, far_rows), BF16),
             pltpu.VMEM((side, block // 2, LANES), BF16),
-            pltpu.VMEM((2 * block, side * block), F32),
-            pltpu.VMEM((2 * block, side * block), BF16),
-            pltpu.VMEM((2 * block, LANES), F32),
+            pltpu.VMEM((block, near_rows), F32),
+            pltpu.VMEM((block, far_rows), F32),
+            pltpu.VMEM((block, near_rows), BF16),
+            pltpu.VMEM((block, far_rows), BF16),
+            pltpu.VMEM((block, LANES), F32),
+            pltpu.VMEM((near_rows // block, block, 2 * LANES), F32),
+            pltpu.VMEM((near_rows // block, block, LANES), F32),
             pltpu.VMEM((side, block, LANES), BF16),
             pltpu.VMEM((side, block, LANES), BF16),
             pltpu.VMEM((groups, WINDOW // 2, LANES), BF16),
@@ -555,7 +632,8 @@
             pltpu.VMEM((2, HALO, width), BF16),
             pltpu.VMEM((2, HALO, width), BF16),
             pltpu.VMEM((rows + 2 * HALO, width), F32),
-            dma((9,)),
+            dma((12,)),
+            dma((2,)),
             dma((groups,)),
             dma((groups,)),
             dma((side,)),
@@ -572,11 +650,14 @@
             dma((2,)),
         ],
         compiler_params=pltpu.CompilerParams(
-            collective_id=0, has_side_effects=True, vmem_limit_bytes=55160 * 1024
+            collective_id=0, has_side_effects=True, vmem_limit_bytes=60 * 1024 * 1024
         ),
     )(
         frames,
-        jnp.stack([attn_gain, conv_gain, bn_scale, bn_shift]),
+        attn_gain.reshape(1, width),
+        conv_gain.reshape(1, width),
+        bn_scale.reshape(1, width),
+        bn_shift.reshape(1, width),
         kernel,
         w_query,
         w_key,
@@ -588,10 +669,10 @@
     return pl.pallas_call(
         copy_kernel,
         out_shape=tuple(jax.ShapeDtypeStruct(r.shape, r.dtype) for r in results),
-        in_specs=[vmem] * 2,
+        in_specs=[anywhere] * 2,
         out_specs=(anywhere, anywhere),
-        scratch_shapes=[dma((2,))],
-        compiler_params=pltpu.CompilerParams(vmem_limit_bytes=4 * 1024 * 1024),
+        scratch_shapes=[pltpu.VMEM((rows, width), BF16), pltpu.VMEM((rows, width), BF16), dma((4,))],
+        compiler_params=pltpu.CompilerParams(vmem_limit_bytes=60 * 1024 * 1024),
     )(*results)
 
 

time: 48 us -> 47.3 us (0.985)
  Pallas kernels: 45.7 us -> 46.5 us
  other arithmetic: 0.69 us -> 0 us
  local copies, waits for them, and re-layouts: 0.69 us -> 0 us
    pallas_call x1, Pallas kernels: 0.64 us -> 1.4 us  [on_device(): pl.pallas_call(copy_kernel, out_shape=tuple((jax.ShapeDtypeStruct(r.shape...]
    another operation x1 -> x0, other arithmetic: 0.69 us -> none  [on_device(): jnp.stack([attn_gain, conv_gain, bn_scale, bn_shift])]
    unnamed x6 -> x0, local copies, waits for them, and re-layouts: 0.69 us -> none
where the time goes in v3:
time: 47.3 us; the launch traced here: 47.1 us
  Pallas kernels  46.5 us (98%)
  between operations  0.64 us (1%)
    pallas_call x1, Pallas kernels, on_device(): pl.pallas_call(functools.partial(layer_kernel, side), out_shape=(jax.Shap...  45.1 us
    pallas_call x1, Pallas kernels, on_device(): pl.pallas_call(copy_kernel, out_shape=tuple((jax.ShapeDtypeStruct(r.shape...  1.4 us

profile of v3, /device:TPU:1, one launch (start us, length us, event | category | flops | bytes accessed | tf_op | source)
XLA Modules:
  0.0 47.1 jit_solution(13740447679429746671)
XLA Ops:
  0.6 45.1 %shard_map.131 = (bf16[24,512]{1,0:T(8,128)(2,1)}, bf16[24,512]{1,0:T(8,128)(2,1)}) custom-call(bf16[24,512]{1,0:T(8,128)(2,1)} %frames_hbm.1, f32[1,512]{1,0:T(1,128)} %bitcast.4, f32[1,512]{1,0:T(1,128)} %bitcast.5, f32[1,512]{1,0:T(1,128)} %bitcast.6, f32[1,512]{1,0:T(1,128)} %bitcast.7, f32[31,512]{1,0:T(8,128)} %taps_hbm.1, ...), custom_call_target="tpu_custom_call" | custom-call | tf_op jit(solution)/shard_map/pallas_call | solution.py:590
  45.7 1.4 %shard_map.132 = (bf16[24,512]{1,0:T(8,128)(2,1)}, bf16[24,512]{1,0:T(8,128)(2,1)}) custom-call(bf16[24,512]{1,0:T(8,128)(2,1)} %get-tuple-element.4.attended_in, bf16[24,512]{1,0:T(8,128)(2,1)} %get-tuple-element.5.layer_in), custom_call_target="tpu_custom_call" | custom-call | tf_op jit(solution)/shard_map/pallas_call | solution.py:669

commit v4 on v3

--- a/solution.py
+++ b/solution.py
@@ -33,7 +33,7 @@
 def folded(rows):
     half = rows.shape[0] // 2
     lane = lax.broadcasted_iota(jnp.int32, (half, LANES), 1)
-    return jnp.where(lane < HEAD_DIM, pltpu.roll(rows[:half], HEAD_DIM, 1), rows[half:]).astype(BF16)
+    return jnp.where(lane < HEAD_DIM, pltpu.roll(rows[:half], HEAD_DIM, 1), rows[half:])
 
 
 def all_heads(ref):
@@ -121,34 +121,37 @@
     groups = head_send.shape[0]
     block = rows * groups
     half_block = block // 2
+    level_rows = -(-block // LANES)
     blocks = side * side
     tm = lax.axis_index("tm")
     kv = lax.axis_index("kv")
-    core = kv % 2
-    slow = tm // side
-    fast = tm % side
+    bits = side.bit_length() - 1
+    core = kv & 1
+    slow = tm >> bits
+    fast = tm & (side - 1)
     key_at = fast + core * (slow - fast)
     key_stride = 1 + core * (side - 1)
     query_at = slow + core * (fast - slow)
     query_stride = side - core * (side - 1)
 
     def kv_peer(d):
-        return (tm, (kv + d) % groups)
+        return (tm, (kv + d) & (groups - 1))
 
     def key_peer(d):
-        return (tm + ((key_at + d) % side - key_at) * key_stride, kv)
+        return (tm + (((key_at + d) & (side - 1)) - key_at) * key_stride, kv)
 
     def query_peer(d):
-        return (tm + ((query_at + d) % side - query_at) * query_stride, kv)
+        return (tm + (((query_at + d) & (side - 1)) - query_at) * query_stride, kv)
 
     devices = groups * blocks
     me = tm * groups + kv
-    following = (me + 1) % devices
-    preceding = (me + devices - 1) % devices
-    following = (following // groups, following % groups)
-    preceding = (preceding // groups, preceding % groups)
-    later = (tm + 1) % blocks
-    earlier = (tm + blocks - 1) % blocks
+    following = (me + 1) & (devices - 1)
+    preceding = (me - 1) & (devices - 1)
+    group_bits = groups.bit_length() - 1
+    following = (following >> group_bits, following & (groups - 1))
+    preceding = (preceding >> group_bits, preceding & (groups - 1))
+    later = (tm + 1) & (blocks - 1)
+    earlier = (tm - 1) & (blocks - 1)
     near = sorted(range(1, side), key=lambda d: min(d, side - d))
 
     def greet(device):
@@ -243,7 +246,7 @@
 
     head_copies = [
         pltpu.make_async_remote_copy(
-            src_ref=head_send.at[(kv + d) % groups],
+            src_ref=head_send.at[(kv + d) & (groups - 1)],
             dst_ref=head_recv.at[kv],
             send_sem=head_ssem.at[d],
             recv_sem=head_rsem.at[d],
@@ -346,7 +349,6 @@
             keys[:, at] = both.astype(F32).T.astype(BF16)
 
     half_lane = lax.broadcasted_iota(jnp.int32, (half_block, LANES), 1)
-    block_lane = lax.broadcasted_iota(jnp.int32, (block, LANES), 1)
 
     def unfolded(d):
         packed = q_all[d].astype(F32)
@@ -374,11 +376,18 @@
     def finish(d, mixed):
         total = mixed[:, LANES:]
         level = tops[...] + jnp.log2(total)
-        high = level.astype(BF16).astype(F32)
-        part_send[d] = jnp.where(
-            block_lane >= HEAD_DIM,
-            mixed[:, :LANES] / total,
-            jnp.where(block_lane < HALF, high, level - high),
+        place = lax.broadcasted_iota(jnp.int32, (HALO, LANES), 0)
+        levels = jnp.zeros((HALO, LANES), F32)
+        for i in range(level_rows):
+            few = level[i * LANES : (i + 1) * LANES]
+            row = lax.broadcasted_iota(jnp.int32, few.shape, 0)
+            column = lax.broadcasted_iota(jnp.int32, few.shape, 1)
+            line = jnp.sum(jnp.where(row == column, few, 0.0), axis=0, keepdims=True)
+            high = line.astype(BF16).astype(F32)
+            levels = jnp.where(place == i, high, levels)
+            levels = jnp.where(place == level_rows + i, line - high, levels)
+        part_send[d] = jnp.concatenate(
+            [folded(mixed[:, :LANES] / total), levels], axis=0
         ).astype(BF16)
 
     def chosen(step, order):
@@ -436,22 +445,62 @@
     for d in range(1, side):
         part_copy(d).wait_recv()
 
-    parts = part_recv[...].reshape(side * block, LANES)
-    pick = lax.broadcasted_iota(jnp.int32, (LANES, LANES), 0)
-    pick = jnp.where((pick == 0) | (pick == HALF), 1.0, 0.0).astype(BF16)
-    levels = matmul(parts, pick).reshape(side, block, LANES)
-    parts = parts.astype(F32).reshape(side, block, LANES)
-    fades = jnp.exp2(levels - jnp.max(levels, axis=0, keepdims=True))
-    merged = jnp.sum(fades * parts, axis=0) / jnp.sum(fades, axis=0)
-
-    edge_send[0] = folded(merged[: 2 * HALO])
-    edge_send[1] = folded(merged[block - 2 * HALO :])
+    levels = []
+    for i in range(level_rows):
+        levels.append(
+            [
+                part_recv[d, half_block + i : half_block + i + 1].astype(F32)
+                + part_recv[d, half_block + level_rows + i : half_block + level_rows + i + 1].astype(F32)
+                for d in range(side)
+            ]
+        )
+    shares = []
+    for level in levels:
+        level = jnp.concatenate(level, axis=0)
+        fade = jnp.exp2(level - jnp.max(level, axis=0, keepdims=True))
+        shares.append(fade / jnp.sum(fade, axis=0, keepdims=True))
+    shares = jnp.concatenate(
+        shares + [jnp.zeros((LANES - side * level_rows, LANES), F32)], axis=0
+    ).T
+    upper = []
+    begin = half_block
+    while begin < block:
+        i = begin // LANES
+        end = min(block, (i + 1) * LANES)
+        few = shares[begin - i * LANES : end - i * LANES]
+        upper.append(pltpu.roll(few, LANES - i * side, 1) if i else few)
+        begin = end
+    lower = shares[:half_block]
+    upper = jnp.concatenate(upper, axis=0)
+    pick = jnp.zeros((half_block, LANES), F32)
+    for i, share in enumerate((lower, upper)):
+        high = share.astype(BF16).astype(F32)
+        for j, piece in enumerate((high, share - high)):
+            begin = (2 * i + j) * side
+            piece = pltpu.roll(piece, begin, 1) if begin else piece
+            pick = jnp.where((half_lane >= begin) & (half_lane < begin + side), piece, pick)
+    index = lax.broadcasted_iota(jnp.int32, (LANES, side * LANES), 0)
+    lane = lax.broadcasted_iota(jnp.int32, (LANES, side * LANES), 1)
+    spread = (
+        (index % side == lane // LANES)
+        & (index < 4 * side)
+        & (index // (2 * side) == lane % LANES // HEAD_DIM)
+    )
+    spread = matmul(pick.astype(BF16), jnp.where(spread, 1.0, 0.0).astype(BF16))
+    merged = jnp.zeros((half_block, LANES), F32)
+    for d in range(side):
+        part = part_recv[d].astype(F32)[:half_block]
+        merged = merged + spread[:, d * LANES : (d + 1) * LANES] * part
+    merged = jnp.concatenate([pltpu.roll(merged, HEAD_DIM, 1), merged], axis=0)
+
+    edge_send[0] = folded(merged[: 2 * HALO]).astype(BF16)
+    edge_send[1] = folded(merged[block - 2 * HALO :]).astype(BF16)
     framed = jnp.concatenate(
         [jnp.zeros((HALO, LANES), F32), merged, jnp.zeros((WINDOW - rows - HALO, LANES), F32)],
         axis=0,
     )
     for part in range(groups):
-        ctx_send[part] = folded(framed[part * rows : part * rows + WINDOW])
+        ctx_send[part] = folded(framed[part * rows : part * rows + WINDOW]).astype(BF16)
 
     def edge_copy(i, head):
         return pltpu.make_async_remote_copy(
@@ -467,7 +516,7 @@
         edge_copy(i, kv).start()
     ctx_copies = [
         pltpu.make_async_remote_copy(
-            src_ref=ctx_send.at[(kv + d) % groups],
+            src_ref=ctx_send.at[(kv + d) & (groups - 1)],
             dst_ref=ctx_recv.at[kv],
             send_sem=ctx_ssem.at[d],
             recv_sem=ctx_rsem.at[d],
@@ -622,8 +671,8 @@
             pltpu.VMEM((block, LANES), F32),
             pltpu.VMEM((near_rows // block, block, 2 * LANES), F32),
             pltpu.VMEM((near_rows // block, block, LANES), F32),
-            pltpu.VMEM((side, block, LANES), BF16),
-            pltpu.VMEM((side, block, LANES), BF16),
+            pltpu.VMEM((side, block // 2 + HALO, LANES), BF16),
+            pltpu.VMEM((side, block // 2 + HALO, LANES), BF16),
             pltpu.VMEM((groups, WINDOW // 2, LANES), BF16),
             pltpu.VMEM((groups, WINDOW // 2, LANES), BF16),
             pltpu.VMEM((2, HALO, LANES), BF16),

time: 47.3 us -> 47.3 us (level)
  no operation moved by 1% of the time
where the time goes in v4:
time: 47.3 us; the launch traced here: 47.1 us
  Pallas kernels  46.4 us (98%)
  between operations  0.64 us (1%)
    pallas_call x1, Pallas kernels, on_device(): pl.pallas_call(functools.partial(layer_kernel, side), out_shape=(jax.Shap...  45 us
    pallas_call x1, Pallas kernels, on_device(): pl.pallas_call(copy_kernel, out_shape=tuple((jax.ShapeDtypeStruct(r.shape...  1.4 us

profile of v4, /device:TPU:1, one launch (start us, length us, event | category | flops | bytes accessed | tf_op | source)
XLA Modules:
  0.0 47.1 jit_solution(14400773599321447072)
XLA Ops:
  0.6 45.0 %shard_map.131 = (bf16[24,512]{1,0:T(8,128)(2,1)}, bf16[24,512]{1,0:T(8,128)(2,1)}) custom-call(bf16[24,512]{1,0:T(8,128)(2,1)} %frames_hbm.1, f32[1,512]{1,0:T(1,128)} %bitcast.4, f32[1,512]{1,0:T(1,128)} %bitcast.5, f32[1,512]{1,0:T(1,128)} %bitcast.6, f32[1,512]{1,0:T(1,128)} %bitcast.7, f32[31,512]{1,0:T(8,128)} %taps_hbm.1, ...), custom_call_target="tpu_custom_call" | custom-call | tf_op jit(solution)/shard_map/pallas_call | solution.py:639
  45.7 1.4 %shard_map.132 = (bf16[24,512]{1,0:T(8,128)(2,1)}, bf16[24,512]{1,0:T(8,128)(2,1)}) custom-call(bf16[24,512]{1,0:T(8,128)(2,1)} %get-tuple-element.4.attended_in, bf16[24,512]{1,0:T(8,128)(2,1)} %get-tuple-element.5.layer_in), custom_call_target="tpu_custom_call" | custom-call | tf_op jit(solution)/shard_map/pallas_call | solution.py:718

commit v5 on v4

--- a/solution.py
+++ b/solution.py
@@ -62,8 +62,6 @@
     w_out_hbm,
     w_expand_hbm,
     w_project_hbm,
-    attended_hbm,
-    layer_hbm,
     attended_ref,
     layer_ref,
     frames_ref,
@@ -101,7 +99,6 @@
     halo_recv,
     padded,
     load_sem,
-    store_sem,
     head_ssem,
     head_rsem,
     kv_ssem,
@@ -182,19 +179,9 @@
     barrier = pltpu.get_barrier_semaphore()
     for d in range(1, groups):
         greet(kv_peer(d))
-    for d in range(1, side):
+    for d in near[:4]:
         greet(key_peer(d))
         greet(query_peer(d))
-
-    @pl.when(kv == groups - 1)
-    def _():
-        for head in range(groups):
-            greet((later, head))
-
-    @pl.when(kv == 0)
-    def _():
-        for head in range(groups):
-            greet((earlier, head))
 
     lane = lax.broadcasted_iota(jnp.int32, (rows, LANES), 1)
     low = lane < HEAD_DIM
@@ -242,7 +229,7 @@
             [key_value, jnp.where(low, pltpu.roll(query, HEAD_DIM, 1), 0.0)], axis=0
         ).astype(BF16)
 
-    pl.semaphore_wait(barrier, groups - 1 + 2 * (side - 1) + 2)
+    pl.semaphore_wait(barrier, groups - 1 + 2 * len(near[:4]))
 
     head_copies = [
         pltpu.make_async_remote_copy(
@@ -256,19 +243,6 @@
         for d in range(1, groups)
     ]
     for copy in head_copies:
-        copy.start()
-    halo_copies = [
-        pltpu.make_async_remote_copy(
-            src_ref=halo_send.at[i],
-            dst_ref=halo_recv.at[i],
-            send_sem=halo_ssem.at[i],
-            recv_sem=halo_rsem.at[i],
-            device_id=target,
-            device_id_type=MESH,
-        )
-        for i, target in enumerate((preceding, following))
-    ]
-    for copy in halo_copies:
         copy.start()
     for load in loads[5:]:
         load.start()
@@ -527,7 +501,30 @@
     ]
     for copy in ctx_copies:
         copy.start()
+    halo_copies = [
+        pltpu.make_async_remote_copy(
+            src_ref=halo_send.at[i],
+            dst_ref=halo_recv.at[i],
+            send_sem=halo_ssem.at[i],
+            recv_sem=halo_rsem.at[i],
+            device_id=target,
+            device_id_type=MESH,
+        )
+        for i, target in enumerate((preceding, following))
+    ]
+    for copy in halo_copies:
+        copy.start()
     ctx_recv[kv] = ctx_send[kv]
+    for copy in head_copies:
+        copy.wait_send()
+    for direct, relayed in lines:
+        for copy in direct.values():
+            copy.wait_send()
+        for onward in relayed.values():
+            for copy in onward.values():
+                copy.wait_send()
+    for d in range(1, side):
+        part_copy(d).wait_send()
     for load in loads[5:]:
         load.wait()
     for copy in halo_copies:
@@ -536,6 +533,10 @@
     nearby = jnp.concatenate([halo_recv[1].astype(F32), inputs, halo_recv[0].astype(F32)], axis=0)
     for copy in ctx_copies:
         copy.wait_recv()
+    for copy in ctx_copies + halo_copies:
+        copy.wait_send()
+    for i in range(2):
+        edge_copy(i, kv).wait_send()
     context[...] = all_heads(ctx_recv)[:extent]
 
     @pl.when(kv == 0)
@@ -552,11 +553,6 @@
 
     attended = matmul(context[...].astype(BF16), w_out[...]).astype(BF16).astype(F32)
     attended_ref[...] = attended[HALO : HALO + rows].astype(BF16)
-    stores = [
-        pltpu.make_async_copy(attended_ref, attended_hbm, store_sem.at[0]),
-        pltpu.make_async_copy(layer_ref, layer_hbm, store_sem.at[1]),
-    ]
-    stores[0].start()
     mid = nearby + attended
     conv_in = layer_norm(mid, gains_ref[1:2]).astype(BF16)
     expanded = matmul(conv_in, w_expand[...])
@@ -578,39 +574,16 @@
     batch = depth * gains_ref[2:3] + gains_ref[3:4]
     act = (batch / (1.0 + jnp.exp(-batch))).astype(BF16)
     layer_ref[...] = (mid[HALO : HALO + rows] + matmul(act, w_project[...])).astype(BF16)
-    stores[1].start()
-
-    for copy in head_copies + halo_copies + ctx_copies:
-        copy.wait_send()
-    for d in range(1, side):
-        part_copy(d).wait_send()
-    for direct, relayed in lines:
-        for copy in direct.values():
-            copy.wait_send()
-        for onward in relayed.values():
-            for copy in onward.values():
-                copy.wait_send()
-    for i in range(2):
-        edge_copy(i, kv).wait_send()
-    for store in stores:
-        store.wait()
-
-
-def copy_kernel(attended_in, layer_in, attended_out, layer_out, attended, layer, sem):
-    def copies(step, *pairs):
-        return [
-            pltpu.make_async_copy(source, target, sem.at[2 * step + i])
-            for i, (source, target) in enumerate(pairs)
-        ]
-
-    inward = copies(0, (attended_in, attended), (layer_in, layer))
-    outward = copies(1, (attended, attended_out), (layer, layer_out))
-    for copy in inward:
+
+
+def copy_kernel(attended_in, layer_in, attended_out, layer_out, sem):
+    copies = [
+        pltpu.make_async_copy(attended_in, attended_out, sem.at[0]),
+        pltpu.make_async_copy(layer_in, layer_out, sem.at[1]),
+    ]
+    for copy in copies:
         copy.start()
-    for copy, onward in zip(inward, outward):
-        copy.wait()
-        onward.start()
-    for copy in outward:
+    for copy in copies:
         copy.wait()
 
 
@@ -634,19 +607,15 @@
     block = rows * groups
     near_rows = (5 if side == 8 else side // 2) * block
     far_rows = side * block - near_rows
+    vmem = pl.BlockSpec(memory_space=pltpu.VMEM)
     anywhere = pl.BlockSpec(memory_space=pl.ANY)
     dma = pltpu.SemaphoreType.DMA
     results = pl.pallas_call(
         functools.partial(layer_kernel, side),
-        out_shape=(
-            jax.ShapeDtypeStruct((rows, width), BF16),
-            jax.ShapeDtypeStruct((rows, width), BF16),
-        ),
+        out_shape=(pltpu.VMEM((rows, width), BF16), pltpu.VMEM((rows, width), BF16)),
         in_specs=[anywhere] * 12,
-        out_specs=(anywhere, anywhere),
+        out_specs=(vmem, vmem),
         scratch_shapes=[
-            pltpu.VMEM((rows, width), BF16),
-            pltpu.VMEM((rows, width), BF16),
             pltpu.VMEM((rows, width), BF16),
             pltpu.VMEM((4, width), F32),
             pltpu.VMEM(kernel.shape, F32),
@@ -682,7 +651,6 @@
             pltpu.VMEM((2, HALO, width), BF16),
             pltpu.VMEM((rows + 2 * HALO, width), F32),
             dma((12,)),
-            dma((2,)),
             dma((groups,)),
             dma((groups,)),
             dma((side,)),
@@ -717,11 +685,11 @@
     )
     return pl.pallas_call(
         copy_kernel,
-        out_shape=tuple(jax.ShapeDtypeStruct(r.shape, r.dtype) for r in results),
-        in_specs=[anywhere] * 2,
+        out_shape=(jax.ShapeDtypeStruct((rows, width), BF16),) * 2,
+        in_specs=[vmem] * 2,
         out_specs=(anywhere, anywhere),
-        scratch_shapes=[pltpu.VMEM((rows, width), BF16), pltpu.VMEM((rows, width), BF16), dma((4,))],
-        compiler_params=pltpu.CompilerParams(vmem_limit_bytes=60 * 1024 * 1024),
+        scratch_shapes=[dma((2,))],
+        compiler_params=pltpu.CompilerParams(vmem_limit_bytes=4 * 1024 * 1024),
     )(*results)
 
 

time: 47.3 us -> 44.9 us (0.949)
  Pallas kernels: 46.4 us -> 44.1 us
    pallas_call x2, Pallas kernels: 46.4 us -> 44.1 us  [the longest x1 43.5 us: on_device(): pl.pallas_call(functools.partial(layer_kernel, side), out_shape=(pltpu.VM...]
where the time goes in v5:
time: 44.9 us; the launch traced here: 44.8 us
  Pallas kernels  44.1 us (98%)
  between operations  0.64 us (1%)
    pallas_call x1, Pallas kernels, on_device(): pl.pallas_call(functools.partial(layer_kernel, side), out_shape=(pltpu.VM...  43.5 us

profile of v5, /device:TPU:1, one launch (start us, length us, event | category | flops | bytes accessed | tf_op | source)
XLA Modules:
  0.0 44.8 jit_solution(13567358506735950524)
XLA Ops:
  0.6 43.5 %shard_map.131 = (bf16[24,512]{1,0:T(8,128)(2,1)S(1)}, bf16[24,512]{1,0:T(8,128)(2,1)S(1)}) custom-call(bf16[24,512]{1,0:T(8,128)(2,1)} %frames_hbm.1, f32[1,512]{1,0:T(1,128)} %bitcast.4, f32[1,512]{1,0:T(1,128)} %bitcast.5, f32[1,512]{1,0:T(1,128)} %bitcast.6, f32[1,512]{1,0:T(1,128)} %bitcast.7, f32[31,512]{1,0:T(8,128)} %taps_hbm.1, ...), custom_call_target="tpu_custom_call" | custom-call | tf_op jit(solution)/shard_map/pallas_call | solution.py:613
  44.1 0.6 %shard_map.132 = (bf16[24,512]{1,0:T(8,128)(2,1)}, bf16[24,512]{1,0:T(8,128)(2,1)}) custom-call(bf16[24,512]{1,0:T(8,128)(2,1)S(1)} %get-tuple-element.4.attended_in, bf16[24,512]{1,0:T(8,128)(2,1)S(1)} %get-tuple-element.5.layer_in), custom_call_target="tpu_custom_call" | custom-call | tf_op jit(solution)/shard_map/pallas_call | solution.py:686

commit v6 on v5

--- a/solution.py
+++ b/solution.py
@@ -247,8 +247,6 @@
     for load in loads[5:]:
         load.start()
     head_recv[kv] = head_send[kv]
-    for wide in (near_wide, far_wide):
-        wide[:, LANES:] = jnp.ones((wide.shape[0], LANES), BF16)
     for copy in head_copies:
         copy.wait_recv()
     pieces = [head_recv[head].astype(F32) for head in range(groups)]
@@ -319,10 +317,13 @@
             few = wanted[i : i + 2]
             both = jnp.concatenate([kv_all[d] for d in few], axis=0)
             at = slice(i * block, (i + len(few)) * block)
-            wide[at, :LANES] = both
-            keys[:, at] = both.astype(F32).T.astype(BF16)
+            both = both.astype(F32)
+            keys[:, at] = both.T.astype(BF16)
+            lane = lax.broadcasted_iota(jnp.int32, both.shape, 1)
+            wide[at] = jnp.where(lane < HEAD_DIM, 1.0, both).astype(BF16)
 
     half_lane = lax.broadcasted_iota(jnp.int32, (half_block, LANES), 1)
+    block_lane = lax.broadcasted_iota(jnp.int32, (block, LANES), 1)
 
     def unfolded(d):
         packed = q_all[d].astype(F32)
@@ -348,7 +349,7 @@
             tops[at] = jnp.broadcast_to(top, (CHUNK, LANES))
 
     def finish(d, mixed):
-        total = mixed[:, LANES:]
+        total = jnp.where(block_lane < HEAD_DIM, mixed, pltpu.roll(mixed, HEAD_DIM, 1))
         level = tops[...] + jnp.log2(total)
         place = lax.broadcasted_iota(jnp.int32, (HALO, LANES), 0)
         levels = jnp.zeros((HALO, LANES), F32)
@@ -361,7 +362,7 @@
             levels = jnp.where(place == i, high, levels)
             levels = jnp.where(place == level_rows + i, line - high, levels)
         part_send[d] = jnp.concatenate(
-            [folded(mixed[:, :LANES] / total), levels], axis=0
+            [folded(mixed / total), levels], axis=0
         ).astype(BF16)
 
     def chosen(step, order):
@@ -407,8 +408,7 @@
         d = chosen(at, near_slots)
         far_scores[...] = matmul(unfolded(d), far_keys[...])
         soften([(far_scores, far_weights)], first_tops.at[at])
-        fade = jnp.exp2(first_tops[at] - tops[...])
-        mixed = first_mixed[at] * jnp.concatenate([fade, fade], axis=1)
+        mixed = first_mixed[at] * jnp.exp2(first_tops[at] - tops[...])
         finish(d, mixed + matmul(far_weights[...], far_wide[...]))
 
         @pl.when(at > 0)
@@ -525,6 +525,10 @@
                 copy.wait_send()
     for d in range(1, side):
         part_copy(d).wait_send()
+    for copy in ctx_copies + halo_copies:
+        copy.wait_send()
+    for i in range(2):
+        edge_copy(i, kv).wait_send()
     for load in loads[5:]:
         load.wait()
     for copy in halo_copies:
@@ -533,10 +537,6 @@
     nearby = jnp.concatenate([halo_recv[1].astype(F32), inputs, halo_recv[0].astype(F32)], axis=0)
     for copy in ctx_copies:
         copy.wait_recv()
-    for copy in ctx_copies + halo_copies:
-        copy.wait_send()
-    for i in range(2):
-        edge_copy(i, kv).wait_send()
     context[...] = all_heads(ctx_recv)[:extent]
 
     @pl.when(kv == 0)
@@ -628,8 +628,8 @@
             pltpu.VMEM((groups, 2 * rows, LANES), BF16),
             pltpu.VMEM((groups, 2 * rows, LANES), BF16),
             pltpu.VMEM((side, block, LANES), BF16),
-            pltpu.VMEM((near_rows, 2 * LANES), BF16),
-            pltpu.VMEM((far_rows, 2 * LANES), BF16),
+            pltpu.VMEM((near_rows, LANES), BF16),
+            pltpu.VMEM((far_rows, LANES), BF16),
             pltpu.VMEM((LANES, near_rows), BF16),
             pltpu.VMEM((LANES, far_rows), BF16),
             pltpu.VMEM((side, block // 2, LANES), BF16),
@@ -638,7 +638,7 @@
             pltpu.VMEM((block, near_rows), BF16),
             pltpu.VMEM((block, far_rows), BF16),
             pltpu.VMEM((block, LANES), F32),
-            pltpu.VMEM((near_rows // block, block, 2 * LANES), F32),
+            pltpu.VMEM((near_rows // block, block, LANES), F32),
             pltpu.VMEM((near_rows // block, block, LANES), F32),
             pltpu.VMEM((side, block // 2 + HALO, LANES), BF16),
             pltpu.VMEM((side, block // 2 + HALO, LANES), BF16),

time: 44.9 us -> 44.7 us (level)
  no operation moved by 1% of the time
where the time goes in v6:
time: 44.7 us; the launch traced here: 44.6 us
  Pallas kernels  43.9 us (98%)
  between operations  0.64 us (1%)
    pallas_call x1, Pallas kernels, on_device(): pl.pallas_call(functools.partial(layer_kernel, side), out_shape=(pltpu.VM...  43.3 us

profile of v6, /device:TPU:1, one launch (start us, length us, event | category | flops | bytes accessed | tf_op | source)
XLA Modules:
  0.0 44.6 jit_solution(8601311643134500054)
XLA Ops:
  0.6 43.3 %shard_map.131 = (bf16[24,512]{1,0:T(8,128)(2,1)S(1)}, bf16[24,512]{1,0:T(8,128)(2,1)S(1)}) custom-call(bf16[24,512]{1,0:T(8,128)(2,1)} %frames_hbm.1, f32[1,512]{1,0:T(1,128)} %bitcast.4, f32[1,512]{1,0:T(1,128)} %bitcast.5, f32[1,512]{1,0:T(1,128)} %bitcast.6, f32[1,512]{1,0:T(1,128)} %bitcast.7, f32[31,512]{1,0:T(8,128)} %taps_hbm.1, ...), custom_call_target="tpu_custom_call" | custom-call | tf_op jit(solution)/shard_map/pallas_call | solution.py:613
  44.0 0.6 %shard_map.132 = (bf16[24,512]{1,0:T(8,128)(2,1)}, bf16[24,512]{1,0:T(8,128)(2,1)}) custom-call(bf16[24,512]{1,0:T(8,128)(2,1)S(1)} %get-tuple-element.4.attended_in, bf16[24,512]{1,0:T(8,128)(2,1)S(1)} %get-tuple-element.5.layer_in), custom_call_target="tpu_custom_call" | custom-call | tf_op jit(solution)/shard_map/pallas_call | solution.py:686

commit v7 on v6

--- a/solution.py
+++ b/solution.py
@@ -293,7 +293,7 @@
     ).astype(BF16)
     for copy in q_direct.values():
         copy.start()
-    for direct, relayed in lines:
+    for direct, relayed in lines[::-1]:
         for d, onward in relayed.items():
             direct[d].wait_recv()
             for copy in onward.values():
@@ -302,15 +302,15 @@
     near_slots = slots[: near_wide.shape[0] // block]
     far_slots = slots[len(near_slots) :]
 
-    def wait_for(wanted):
-        for direct, relayed in lines:
-            for d, copy in direct.items():
-                if d in wanted and d not in relayed:
+    def wait_for(line, wanted):
+        direct, relayed = line
+        for d, copy in direct.items():
+            if d in wanted and d not in relayed:
+                copy.wait_recv()
+        for onward in relayed.values():
+            for d, copy in onward.items():
+                if (d or 4) in wanted:
                     copy.wait_recv()
-            for onward in relayed.values():
-                for d, copy in onward.items():
-                    if (d or 4) in wanted:
-                        copy.wait_recv()
 
     def lay_out(wanted, wide, keys):
         for i in range(0, len(wanted), 2):
@@ -336,7 +336,7 @@
         ).astype(BF16)
 
     def soften(pieces, floor=None):
-        for begin in range(0, block, CHUNK):
+        for begin in range(0, 2 * block, CHUNK):
             at = slice(begin, begin + CHUNK)
             score = [scores[at] for scores, _ in pieces]
             top = functools.reduce(
@@ -348,9 +348,9 @@
                 weights[at] = jnp.exp2(part - top).astype(BF16)
             tops[at] = jnp.broadcast_to(top, (CHUNK, LANES))
 
-    def finish(d, mixed):
+    def finish(d, mixed, top):
         total = jnp.where(block_lane < HEAD_DIM, mixed, pltpu.roll(mixed, HEAD_DIM, 1))
-        level = tops[...] + jnp.log2(total)
+        level = top + jnp.log2(total)
         place = lax.broadcasted_iota(jnp.int32, (HALO, LANES), 0)
         levels = jnp.zeros((HALO, LANES), F32)
         for i in range(level_rows):
@@ -368,17 +368,30 @@
     def chosen(step, order):
         return sum((step == i).astype(jnp.int32) * d for i, d in enumerate(order))
 
-    wait_for(near_slots)
+    steps = side // 2
+    early_steps = len(near_slots) // 2
+
+    def pair_of(step):
+        return chosen(2 * step, slots), chosen(2 * step + 1, slots)
+
+    for line in lines:
+        wait_for(line, near_slots)
     lay_out(near_slots, near_wide, near_keys)
 
-    @pl.loop(0, len(near_slots))
+    @pl.loop(0, steps)
     def _(step):
-        near_scores[...] = matmul(unfolded(chosen(step, near_slots)), near_keys[...])
+        @pl.when(step == early_steps)
+        def _():
+            wait_for(lines[1], far_slots)
+
+        first, second = pair_of(step)
+        query = jnp.concatenate([unfolded(first), unfolded(second)], axis=0)
+        near_scores[...] = matmul(query, near_keys[...])
         soften([(near_scores, near_weights)])
         first_mixed[step] = matmul(near_weights[...], near_wide[...])
         first_tops[step] = tops[...]
 
-    wait_for(far_slots)
+    wait_for(lines[0], far_slots)
     lay_out(far_slots, far_wide, far_keys)
 
     def part_copy(d):
@@ -391,29 +404,22 @@
             device_id_type=MESH,
         )
 
-    @pl.loop(0, len(far_slots))
-    def _(step):
-        d = chosen(step, far_slots[::-1])
-        query = unfolded(d)
-        near_scores[...] = matmul(query, near_keys[...])
+    @pl.loop(0, steps)
+    def _(turn):
+        step = steps - 1 - turn
+        first, second = pair_of(step)
+        query = jnp.concatenate([unfolded(first), unfolded(second)], axis=0)
         far_scores[...] = matmul(query, far_keys[...])
-        soften([(near_scores, near_weights), (far_scores, far_weights)])
-        mixed = matmul(near_weights[...], near_wide[...])
-        finish(d, mixed + matmul(far_weights[...], far_wide[...]))
-        part_copy(d).start()
-
-    @pl.loop(0, len(near_slots))
-    def _(step):
-        at = len(near_slots) - 1 - step
-        d = chosen(at, near_slots)
-        far_scores[...] = matmul(unfolded(d), far_keys[...])
-        soften([(far_scores, far_weights)], first_tops.at[at])
-        mixed = first_mixed[at] * jnp.exp2(first_tops[at] - tops[...])
-        finish(d, mixed + matmul(far_weights[...], far_wide[...]))
-
-        @pl.when(at > 0)
+        soften([(far_scores, far_weights)], first_tops.at[step])
+        mixed = first_mixed[step] * jnp.exp2(first_tops[step] - tops[...])
+        mixed = mixed + matmul(far_weights[...], far_wide[...])
+        finish(second, mixed[block:], tops[block:])
+        part_copy(second).start()
+        finish(first, mixed[:block], tops[:block])
+
+        @pl.when(step > 0)
         def _():
-            part_copy(d).start()
+            part_copy(first).start()
 
     part_recv[0] = part_send[0]
     for d in range(1, side):
@@ -633,13 +639,13 @@
             pltpu.VMEM((LANES, near_rows), BF16),
             pltpu.VMEM((LANES, far_rows), BF16),
             pltpu.VMEM((side, block // 2, LANES), BF16),
-            pltpu.VMEM((block, near_rows), F32),
-            pltpu.VMEM((block, far_rows), F32),
-            pltpu.VMEM((block, near_rows), BF16),
-            pltpu.VMEM((block, far_rows), BF16),
-            pltpu.VMEM((block, LANES), F32),
-            pltpu.VMEM((near_rows // block, block, LANES), F32),
-            pltpu.VMEM((near_rows // block, block, LANES), F32),
+            pltpu.VMEM((2 * block, near_rows), F32),
+            pltpu.VMEM((2 * block, far_rows), F32),
+            pltpu.VMEM((2 * block, near_rows), BF16),
+            pltpu.VMEM((2 * block, far_rows), BF16),
+            pltpu.VMEM((2 * block, LANES), F32),
+            pltpu.VMEM((side // 2, 2 * block, LANES), F32),
+            pltpu.VMEM((side // 2, 2 * block, LANES), F32),
             pltpu.VMEM((side, block // 2 + HALO, LANES), BF16),
             pltpu.VMEM((side, block // 2 + HALO, LANES), BF16),
             pltpu.VMEM((groups, WINDOW // 2, LANES), BF16),

time: 44.7 us -> 43.9 us (0.982)
  Pallas kernels: 43.9 us -> 43.2 us
    pallas_call x1, Pallas kernels: 43.3 us -> 42.5 us  [on_device(): pl.pallas_call(functools.partial(layer_kernel, side), out_shape=(pltpu.VM...]
where the time goes in v7:
time: 43.9 us; the launch traced here: 43.8 us
  Pallas kernels  43.2 us (98%)
  between operations  0.64 us (1%)
    pallas_call x1, Pallas kernels, on_device(): pl.pallas_call(functools.partial(layer_kernel, side), out_shape=(pltpu.VM...  42.5 us

profile of v7, /device:TPU:1, one launch (start us, length us, event | category | flops | bytes accessed | tf_op | source)
XLA Modules:
  0.0 43.8 jit_solution(14532275255248452145)
XLA Ops:
  0.6 42.5 %shard_map.131 = (bf16[24,512]{1,0:T(8,128)(2,1)S(1)}, bf16[24,512]{1,0:T(8,128)(2,1)S(1)}) custom-call(bf16[24,512]{1,0:T(8,128)(2,1)} %frames_hbm.1, f32[1,512]{1,0:T(1,128)} %bitcast.4, f32[1,512]{1,0:T(1,128)} %bitcast.5, f32[1,512]{1,0:T(1,128)} %bitcast.6, f32[1,512]{1,0:T(1,128)} %bitcast.7, f32[31,512]{1,0:T(8,128)} %taps_hbm.1, ...), custom_call_target="tpu_custom_call" | custom-call | tf_op jit(solution)/shard_map/pallas_call | solution.py:619
  43.2 0.6 %shard_map.132 = (bf16[24,512]{1,0:T(8,128)(2,1)}, bf16[24,512]{1,0:T(8,128)(2,1)}) custom-call(bf16[24,512]{1,0:T(8,128)(2,1)S(1)} %get-tuple-element.4.attended_in, bf16[24,512]{1,0:T(8,128)(2,1)S(1)} %get-tuple-element.5.layer_in), custom_call_target="tpu_custom_call" | custom-call | tf_op jit(solution)/shard_map/pallas_call | solution.py:692

commit v8 on v7

--- a/solution.py
+++ b/solution.py
@@ -85,7 +85,7 @@
     far_scores,
     near_weights,
     far_weights,
-    tops,
+    far_tops,
     first_mixed,
     first_tops,
     part_send,
@@ -149,6 +149,7 @@
     preceding = (preceding >> group_bits, preceding & (groups - 1))
     later = (tm + 1) & (blocks - 1)
     earlier = (tm - 1) & (blocks - 1)
+    far_first = sorted(range(1, groups), key=lambda d: -min(d, groups - d))
     near = sorted(range(1, side), key=lambda d: min(d, side - d))
 
     def greet(device):
@@ -240,7 +241,7 @@
             device_id=kv_peer(d),
             device_id_type=MESH,
         )
-        for d in range(1, groups)
+        for d in far_first
     ]
     for copy in head_copies:
         copy.start()
@@ -269,7 +270,7 @@
 
         if side < 8:
             return {d: copy(ref.at[0], ref.at[d], d, d) for d in near}, {}
-        direct = {d: copy(ref.at[0], ref.at[d], d, d) for d in near[:4]}
+        direct = {d: copy(ref.at[0], ref.at[d], d, d) for d in (2, 6, 1, 7)}
         relayed = {
             2: {
                 3: copy(ref.at[2], ref.at[3], 1, 3),
@@ -335,17 +336,14 @@
             axis=0,
         ).astype(BF16)
 
-    def soften(pieces, floor=None):
+    def soften(scores, weights, tops, floor=None):
         for begin in range(0, 2 * block, CHUNK):
             at = slice(begin, begin + CHUNK)
-            score = [scores[at] for scores, _ in pieces]
-            top = functools.reduce(
-                jnp.maximum, [jnp.max(part, axis=1, keepdims=True) for part in score]
-            )
+            score = scores[at]
+            top = jnp.max(score, axis=1, keepdims=True)
             if floor is not None:
                 top = jnp.maximum(top, floor[at, :1])
-            for part, (_, weights) in zip(score, pieces):
-                weights[at] = jnp.exp2(part - top).astype(BF16)
+            weights[at] = jnp.exp2(score - top).astype(BF16)
             tops[at] = jnp.broadcast_to(top, (CHUNK, LANES))
 
     def finish(d, mixed, top):
@@ -387,9 +385,8 @@
         first, second = pair_of(step)
         query = jnp.concatenate([unfolded(first), unfolded(second)], axis=0)
         near_scores[...] = matmul(query, near_keys[...])
-        soften([(near_scores, near_weights)])
+        soften(near_scores, near_weights, first_tops.at[step])
         first_mixed[step] = matmul(near_weights[...], near_wide[...])
-        first_tops[step] = tops[...]
 
     wait_for(lines[0], far_slots)
     lay_out(far_slots, far_wide, far_keys)
@@ -404,22 +401,26 @@
             device_id_type=MESH,
         )
 
-    @pl.loop(0, steps)
-    def _(turn):
-        step = steps - 1 - turn
-        first, second = pair_of(step)
-        query = jnp.concatenate([unfolded(first), unfolded(second)], axis=0)
-        far_scores[...] = matmul(query, far_keys[...])
-        soften([(far_scores, far_weights)], first_tops.at[step])
-        mixed = first_mixed[step] * jnp.exp2(first_tops[step] - tops[...])
-        mixed = mixed + matmul(far_weights[...], far_wide[...])
-        finish(second, mixed[block:], tops[block:])
-        part_copy(second).start()
-        finish(first, mixed[:block], tops[:block])
-
-        @pl.when(step > 0)
-        def _():
-            part_copy(first).start()
+    pairs = [tuple(slots[2 * step : 2 * step + 2]) for step in range(steps)]
+
+    def score_far(step):
+        query = jnp.concatenate([unfolded(d) for d in pairs[step]], axis=0)
+        far_scores[step] = matmul(query, far_keys[...])
+
+    score_far(steps - 1)
+    for step in range(steps - 1, -1, -1):
+        if step > 0:
+            score_far(step - 1)
+        soften(far_scores.at[step], far_weights.at[step], far_tops.at[step], first_tops.at[step])
+        top = far_tops[step]
+        mixed = first_mixed[step] * jnp.exp2(first_tops[step] - top)
+        mixed = mixed + matmul(far_weights[step], far_wide[...])
+        for i in (1, 0):
+            d = pairs[step][i]
+            at = slice(i * block, (i + 1) * block)
+            finish(d, mixed[at], top[at])
+            if d > 0:
+                part_copy(d).start()
 
     part_recv[0] = part_send[0]
     for d in range(1, side):
@@ -503,7 +504,7 @@
             device_id=kv_peer(d),
             device_id_type=MESH,
         )
-        for d in range(1, groups)
+        for d in far_first
     ]
     for copy in ctx_copies:
         copy.start()
@@ -640,10 +641,10 @@
             pltpu.VMEM((LANES, far_rows), BF16),
             pltpu.VMEM((side, block // 2, LANES), BF16),
             pltpu.VMEM((2 * block, near_rows), F32),
-            pltpu.VMEM((2 * block, far_rows), F32),
+            pltpu.VMEM((side // 2, 2 * block, far_rows), F32),
             pltpu.VMEM((2 * block, near_rows), BF16),
-            pltpu.VMEM((2 * block, far_rows), BF16),
-            pltpu.VMEM((2 * block, LANES), F32),
+            pltpu.VMEM((side // 2, 2 * block, far_rows), BF16),
+            pltpu.VMEM((side // 2, 2 * block, LANES), F32),
             pltpu.VMEM((side // 2, 2 * block, LANES), F32),
             pltpu.VMEM((side // 2, 2 * block, LANES), F32),
             pltpu.VMEM((side, block // 2 + HALO, LANES), BF16),

time: 43.9 us -> 42.6 us (0.970)
  Pallas kernels: 43.2 us -> 41.8 us
    pallas_call x1, Pallas kernels: 42.5 us -> 41.1 us  [on_device(): pl.pallas_call(functools.partial(layer_kernel, side), out_shape=(pltpu.VM...]
where the time goes in v8:
time: 42.6 us; the launch traced here: 42.4 us
  Pallas kernels  41.8 us (98%)
  between operations  0.64 us (2%)
    pallas_call x1, Pallas kernels, on_device(): pl.pallas_call(functools.partial(layer_kernel, side), out_shape=(pltpu.VM...  41.1 us

profile of v8, /device:TPU:1, one launch (start us, length us, event | category | flops | bytes accessed | tf_op | source)
XLA Modules:
  0.0 42.4 jit_solution(3137043900671618444)
XLA Ops:
  0.6 41.1 %shard_map.131 = (bf16[24,512]{1,0:T(8,128)(2,1)S(1)}, bf16[24,512]{1,0:T(8,128)(2,1)S(1)}) custom-call(bf16[24,512]{1,0:T(8,128)(2,1)} %frames_hbm.1, f32[1,512]{1,0:T(1,128)} %bitcast.4, f32[1,512]{1,0:T(1,128)} %bitcast.5, f32[1,512]{1,0:T(1,128)} %bitcast.6, f32[1,512]{1,0:T(1,128)} %bitcast.7, f32[31,512]{1,0:T(8,128)} %taps_hbm.1, ...), custom_call_target="tpu_custom_call" | custom-call | tf_op jit(solution)/shard_map/pallas_call | solution.py:620
  41.8 0.6 %shard_map.132 = (bf16[24,512]{1,0:T(8,128)(2,1)}, bf16[24,512]{1,0:T(8,128)(2,1)}) custom-call(bf16[24,512]{1,0:T(8,128)(2,1)S(1)} %get-tuple-element.4.attended_in, bf16[24,512]{1,0:T(8,128)(2,1)S(1)} %get-tuple-element.5.layer_in), custom_call_target="tpu_custom_call" | custom-call | tf_op jit(solution)/shard_map/pallas_call | solution.py:693

commit v9 on v8

--- a/solution.py
+++ b/solution.py
@@ -254,74 +254,85 @@
     own_block = jnp.concatenate([piece[:rows] for piece in pieces], axis=0).astype(BF16)
     kv_all[0] = own_block
 
-    def line_copies(ref, ssem, rsem, peer):
+    def line_copies(ref, ssem, rsem, peer, halved):
         half = ref.shape[1] // 2
-        lower, upper = pl.ds(0, half), pl.ds(half, half)
-
-        def copy(source, target, place, sem):
+        lower, upper, whole = pl.ds(0, half), pl.ds(half, half), pl.ds(0, 2 * half)
+        used = []
+
+        def copy(source, target, rows, place):
+            sem = len(used)
+            used.append(sem)
             return pltpu.make_async_remote_copy(
-                src_ref=source,
-                dst_ref=target,
+                src_ref=ref.at[source, rows],
+                dst_ref=ref.at[target, rows],
                 send_sem=ssem.at[sem],
                 recv_sem=rsem.at[sem],
                 device_id=peer(place),
                 device_id_type=MESH,
             )
 
+        def entry(place, rows, onward=()):
+            return place, copy(0, place, rows, place), [
+                (target, copy(place, target, rows, step)) for target, rows, step in onward
+            ]
+
         if side < 8:
-            return {d: copy(ref.at[0], ref.at[d], d, d) for d in near}, {}
-        direct = {d: copy(ref.at[0], ref.at[d], d, d) for d in (2, 6, 1, 7)}
-        relayed = {
-            2: {
-                3: copy(ref.at[2], ref.at[3], 1, 3),
-                4: copy(ref.at[2, lower], ref.at[4, lower], 2, 4),
-            },
-            6: {
-                5: copy(ref.at[6], ref.at[5], 7, 5),
-                0: copy(ref.at[6, upper], ref.at[4, upper], 6, 0),
-            },
-        }
-        return direct, relayed
-
-    kv_direct, kv_relayed = line_copies(kv_all, kv_ssem, kv_rsem, key_peer)
-    q_direct, q_relayed = line_copies(q_all, q_ssem, q_rsem, query_peer)
-    lines = ((kv_direct, kv_relayed), (q_direct, q_relayed))
-    for copy in kv_direct.values():
+            return [entry(d, whole) for d in near]
+        if halved:
+            return [
+                entry(2, lower, [(4, lower, 2), (3, lower, 1)]),
+                entry(6, upper, [(4, upper, 6), (5, upper, 7)]),
+                entry(2, upper, [(3, upper, 1)]),
+                entry(6, lower, [(5, lower, 7)]),
+                entry(1, whole),
+                entry(7, whole),
+            ]
+        return [
+            entry(2, whole, [(4, lower, 2), (3, whole, 1)]),
+            entry(6, whole, [(4, upper, 6), (5, whole, 7)]),
+            entry(1, whole),
+            entry(7, whole),
+        ]
+
+    kv_line = line_copies(kv_all, kv_ssem, kv_rsem, key_peer, True)
+    q_line = line_copies(q_all, q_ssem, q_rsem, query_peer, False)
+    for _, copy, _ in kv_line:
         copy.start()
     own_queries = jnp.concatenate([piece[rows:] for piece in pieces], axis=0)
     q_all[0] = (
         own_queries[:half_block] + pltpu.roll(own_queries[half_block:], HEAD_DIM, 1)
     ).astype(BF16)
-    for copy in q_direct.values():
+    for _, copy, _ in q_line:
         copy.start()
-    for direct, relayed in lines[::-1]:
-        for d, onward in relayed.items():
-            direct[d].wait_recv()
-            for copy in onward.values():
-                copy.start()
+    for line in (q_line, kv_line):
+        for _, copy, onward in line:
+            if onward:
+                copy.wait_recv()
+            for _, relay in onward:
+                relay.start()
+
     slots = [0] + near
-    near_slots = slots[: near_wide.shape[0] // block]
-    far_slots = slots[len(near_slots) :]
+    near_count = near_wide.shape[0] // block
 
     def wait_for(line, wanted):
-        direct, relayed = line
-        for d, copy in direct.items():
-            if d in wanted and d not in relayed:
+        for slot, copy, onward in line:
+            if slot in wanted and not onward:
                 copy.wait_recv()
-        for onward in relayed.values():
-            for d, copy in onward.items():
-                if (d or 4) in wanted:
-                    copy.wait_recv()
-
-    def lay_out(wanted, wide, keys):
-        for i in range(0, len(wanted), 2):
-            few = wanted[i : i + 2]
-            both = jnp.concatenate([kv_all[d] for d in few], axis=0)
-            at = slice(i * block, (i + len(few)) * block)
-            both = both.astype(F32)
-            keys[:, at] = both.T.astype(BF16)
-            lane = lax.broadcasted_iota(jnp.int32, both.shape, 1)
-            wide[at] = jnp.where(lane < HEAD_DIM, 1.0, both).astype(BF16)
+            for target, relay in onward:
+                if target in wanted:
+                    relay.wait_recv()
+
+    def lay_out(few, at, wide, keys):
+        both = jnp.concatenate([kv_all[d] for d in few], axis=0).astype(F32)
+        at = slice(at * block, (at + len(few)) * block)
+        keys[:, at] = both.T.astype(BF16)
+        lane = lax.broadcasted_iota(jnp.int32, both.shape, 1)
+        wide[at] = jnp.where(lane < HEAD_DIM, 1.0, both).astype(BF16)
+
+    def lay_out_line(kv_slots, wide, keys):
+        for i in range(0, len(kv_slots), 2):
+            wait_for(kv_line, kv_slots[i : i + 2])
+            lay_out(kv_slots[i : i + 2], i, wide, keys)
 
     half_lane = lax.broadcasted_iota(jnp.int32, (half_block, LANES), 1)
     block_lane = lax.broadcasted_iota(jnp.int32, (block, LANES), 1)
@@ -367,29 +378,29 @@
         return sum((step == i).astype(jnp.int32) * d for i, d in enumerate(order))
 
     steps = side // 2
-    early_steps = len(near_slots) // 2
-
-    def pair_of(step):
-        return chosen(2 * step, slots), chosen(2 * step + 1, slots)
-
-    for line in lines:
-        wait_for(line, near_slots)
-    lay_out(near_slots, near_wide, near_keys)
-
-    @pl.loop(0, steps)
-    def _(step):
-        @pl.when(step == early_steps)
+    pairs = [tuple(slots[2 * step : 2 * step + 2]) for step in range(steps)]
+    near_order = [2, 6, 1, 7, 0] if side == 8 else slots[:near_count]
+    far_order = slots[near_count:]
+    wait_for(q_line, slots[:near_count])
+    lay_out_line(near_order, near_wide, near_keys)
+
+    @pl.loop(0, max(steps // 2, 1))
+    def _(turn):
+        @pl.when(turn == steps // 4)
         def _():
-            wait_for(lines[1], far_slots)
-
-        first, second = pair_of(step)
-        query = jnp.concatenate([unfolded(first), unfolded(second)], axis=0)
-        near_scores[...] = matmul(query, near_keys[...])
-        soften(near_scores, near_weights, first_tops.at[step])
-        first_mixed[step] = matmul(near_weights[...], near_wide[...])
-
-    wait_for(lines[0], far_slots)
-    lay_out(far_slots, far_wide, far_keys)
+            wait_for(q_line, far_order)
+
+        ahead = min(2, steps)
+        for i in range(ahead):
+            step = ahead * turn + i
+            query = [unfolded(chosen(2 * step + j, slots)) for j in range(2)]
+            near_scores[i] = matmul(jnp.concatenate(query, axis=0), near_keys[...])
+        for i in range(ahead):
+            step = ahead * turn + i
+            soften(near_scores.at[i], near_weights.at[i], first_tops.at[step])
+            first_mixed[step] = matmul(near_weights[i], near_wide[...])
+
+    lay_out_line(far_order, far_wide, far_keys)
 
     def part_copy(d):
         return pltpu.make_async_remote_copy(
@@ -400,8 +411,6 @@
             device_id=query_peer(side - d),
             device_id_type=MESH,
         )
-
-    pairs = [tuple(slots[2 * step : 2 * step + 2]) for step in range(steps)]
 
     def score_far(step):
         query = jnp.concatenate([unfolded(d) for d in pairs[step]], axis=0)
@@ -524,12 +533,11 @@
     ctx_recv[kv] = ctx_send[kv]
     for copy in head_copies:
         copy.wait_send()
-    for direct, relayed in lines:
-        for copy in direct.values():
+    for line in (kv_line, q_line):
+        for _, copy, onward in line:
             copy.wait_send()
-        for onward in relayed.values():
-            for copy in onward.values():
-                copy.wait_send()
+            for _, relay in onward:
+                relay.wait_send()
     for d in range(1, side):
         part_copy(d).wait_send()
     for copy in ctx_copies + halo_copies:
@@ -640,9 +648,9 @@
             pltpu.VMEM((LANES, near_rows), BF16),
             pltpu.VMEM((LANES, far_rows), BF16),
             pltpu.VMEM((side, block // 2, LANES), BF16),
-            pltpu.VMEM((2 * block, near_rows), F32),
+            pltpu.VMEM((2, 2 * block, near_rows), F32),
             pltpu.VMEM((side // 2, 2 * block, far_rows), F32),
-            pltpu.VMEM((2 * block, near_rows), BF16),
+            pltpu.VMEM((2, 2 * block, near_rows), BF16),
             pltpu.VMEM((side // 2, 2 * block, far_rows), BF16),
             pltpu.VMEM((side // 2, 2 * block, LANES), F32),
             pltpu.VMEM((side // 2, 2 * block, LANES), F32),
@@ -660,8 +668,8 @@
             dma((12,)),
             dma((groups,)),
             dma((groups,)),
-            dma((side,)),
-            dma((side,)),
+            dma((2 * side,)),
+            dma((2 * side,)),
             dma((side,)),
             dma((side,)),
             dma((side,)),

time: 42.6 us -> 41.8 us (0.981)
  Pallas kernels: 41.8 us -> 41 us
    pallas_call x1, Pallas kernels: 41.1 us -> 40.3 us  [on_device(): pl.pallas_call(functools.partial(layer_kernel, side), out_shape=(pltpu.VM...]
where the time goes in v9:
time: 41.8 us; the launch traced here: 41.6 us
  Pallas kernels  41 us (98%)
  between operations  0.64 us (2%)
    pallas_call x1, Pallas kernels, on_device(): pl.pallas_call(functools.partial(layer_kernel, side), out_shape=(pltpu.VM...  40.3 us

profile of v9, /device:TPU:1, one launch (start us, length us, event | category | flops | bytes accessed | tf_op | source)
XLA Modules:
  0.0 41.6 jit_solution(12453679949079537677)
XLA Ops:
  0.6 40.3 %shard_map.131 = (bf16[24,512]{1,0:T(8,128)(2,1)S(1)}, bf16[24,512]{1,0:T(8,128)(2,1)S(1)}) custom-call(bf16[24,512]{1,0:T(8,128)(2,1)} %frames_hbm.1, f32[1,512]{1,0:T(1,128)} %bitcast.4, f32[1,512]{1,0:T(1,128)} %bitcast.5, f32[1,512]{1,0:T(1,128)} %bitcast.6, f32[1,512]{1,0:T(1,128)} %bitcast.7, f32[31,512]{1,0:T(8,128)} %taps_hbm.1, ...), custom_call_target="tpu_custom_call" | custom-call | tf_op jit(solution)/shard_map/pallas_call | solution.py:628
  41.0 0.6 %shard_map.132 = (bf16[24,512]{1,0:T(8,128)(2,1)}, bf16[24,512]{1,0:T(8,128)(2,1)}) custom-call(bf16[24,512]{1,0:T(8,128)(2,1)S(1)} %get-tuple-element.4.attended_in, bf16[24,512]{1,0:T(8,128)(2,1)S(1)} %get-tuple-element.5.layer_in), custom_call_target="tpu_custom_call" | custom-call | tf_op jit(solution)/shard_map/pallas_call | solution.py:701

commit v10 on v9

--- a/solution.py
+++ b/solution.py
@@ -360,19 +360,21 @@
     def finish(d, mixed, top):
         total = jnp.where(block_lane < HEAD_DIM, mixed, pltpu.roll(mixed, HEAD_DIM, 1))
         level = top + jnp.log2(total)
-        place = lax.broadcasted_iota(jnp.int32, (HALO, LANES), 0)
-        levels = jnp.zeros((HALO, LANES), F32)
+        place = lax.broadcasted_iota(jnp.int32, (part_send.shape[1] - half_block, LANES), 0)
+        levels = jnp.zeros(place.shape, F32)
         for i in range(level_rows):
             few = level[i * LANES : (i + 1) * LANES]
             row = lax.broadcasted_iota(jnp.int32, few.shape, 0)
             column = lax.broadcasted_iota(jnp.int32, few.shape, 1)
             line = jnp.sum(jnp.where(row == column, few, 0.0), axis=0, keepdims=True)
             high = line.astype(BF16).astype(F32)
-            levels = jnp.where(place == i, high, levels)
-            levels = jnp.where(place == level_rows + i, line - high, levels)
-        part_send[d] = jnp.concatenate(
-            [folded(mixed / total), levels], axis=0
-        ).astype(BF16)
+            levels = jnp.where(place == i * side + d, high, levels)
+            levels = jnp.where(place == (level_rows + i) * side + d, line - high, levels)
+        part = jnp.concatenate([folded(mixed / total), levels], axis=0).astype(BF16)
+        if d > 0:
+            part_send[d] = part
+        else:
+            part_recv[d] = part
 
     def chosen(step, order):
         return sum((step == i).astype(jnp.int32) * d for i, d in enumerate(order))
@@ -416,10 +418,11 @@
         query = jnp.concatenate([unfolded(d) for d in pairs[step]], axis=0)
         far_scores[step] = matmul(query, far_keys[...])
 
-    score_far(steps - 1)
-    for step in range(steps - 1, -1, -1):
-        if step > 0:
-            score_far(step - 1)
+    turns = [1, 3, 2, 0] if side == 8 else list(range(steps))[::-1]
+    score_far(turns[0])
+    for step, following_step in zip(turns, turns[1:] + [None]):
+        if following_step is not None:
+            score_far(following_step)
         soften(far_scores.at[step], far_weights.at[step], far_tops.at[step], first_tops.at[step])
         top = far_tops[step]
         mixed = first_mixed[step] * jnp.exp2(first_tops[step] - top)
@@ -431,22 +434,16 @@
             if d > 0:
                 part_copy(d).start()
 
-    part_recv[0] = part_send[0]
     for d in range(1, side):
         part_copy(d).wait_recv()
 
-    levels = []
+    levels = part_recv[0].astype(F32)[half_block:]
+    for d in range(1, side):
+        levels = levels + part_recv[d].astype(F32)[half_block:]
+    shares = []
     for i in range(level_rows):
-        levels.append(
-            [
-                part_recv[d, half_block + i : half_block + i + 1].astype(F32)
-                + part_recv[d, half_block + level_rows + i : half_block + level_rows + i + 1].astype(F32)
-                for d in range(side)
-            ]
-        )
-    shares = []
-    for level in levels:
-        level = jnp.concatenate(level, axis=0)
+        high, low = [levels[(j * level_rows + i) * side : (j * level_rows + i + 1) * side] for j in range(2)]
+        level = high + low
         fade = jnp.exp2(level - jnp.max(level, axis=0, keepdims=True))
         shares.append(fade / jnp.sum(fade, axis=0, keepdims=True))
     shares = jnp.concatenate(
@@ -622,6 +619,7 @@
     block = rows * groups
     near_rows = (5 if side == 8 else side // 2) * block
     far_rows = side * block - near_rows
+    part_rows = block // 2 + -(-2 * side * -(-block // LANES) // HALO) * HALO
     vmem = pl.BlockSpec(memory_space=pltpu.VMEM)
     anywhere = pl.BlockSpec(memory_space=pl.ANY)
     dma = pltpu.SemaphoreType.DMA
@@ -655,8 +653,8 @@
             pltpu.VMEM((side // 2, 2 * block, LANES), F32),
             pltpu.VMEM((side // 2, 2 * block, LANES), F32),
             pltpu.VMEM((side // 2, 2 * block, LANES), F32),
-            pltpu.VMEM((side, block // 2 + HALO, LANES), BF16),
-            pltpu.VMEM((side, block // 2 + HALO, LANES), BF16),
+            pltpu.VMEM((side, part_rows, LANES), BF16),
+            pltpu.VMEM((side, part_rows, LANES), BF16),
             pltpu.VMEM((groups, WINDOW // 2, LANES), BF16),
             pltpu.VMEM((groups, WINDOW // 2, LANES), BF16),
             pltpu.VMEM((2, HALO, LANES), BF16),

time: 41.8 us -> 42.5 us (1.017)
  Pallas kernels: 41 us -> 41.7 us
    pallas_call x1, Pallas kernels: 40.3 us -> 41.1 us  [on_device(): pl.pallas_call(functools.partial(layer_kernel, side), out_shape=(pltpu.VM...]
where the time goes in v10:
time: 42.5 us; the launch traced here: 42.4 us
  Pallas kernels  41.7 us (98%)
  between operations  0.64 us (2%)
    pallas_call x1, Pallas kernels, on_device(): pl.pallas_call(functools.partial(layer_kernel, side), out_shape=(pltpu.VM...  41.1 us

profile of v10, /device:TPU:1, one launch (start us, length us, event | category | flops | bytes accessed | tf_op | source)
XLA Modules:
  0.0 42.4 jit_solution(5782676589253907972)
XLA Ops:
  0.6 41.1 %shard_map.131 = (bf16[24,512]{1,0:T(8,128)(2,1)S(1)}, bf16[24,512]{1,0:T(8,128)(2,1)S(1)}) custom-call(bf16[24,512]{1,0:T(8,128)(2,1)} %frames_hbm.1, f32[1,512]{1,0:T(1,128)} %bitcast.4, f32[1,512]{1,0:T(1,128)} %bitcast.5, f32[1,512]{1,0:T(1,128)} %bitcast.6, f32[1,512]{1,0:T(1,128)} %bitcast.7, f32[31,512]{1,0:T(8,128)} %taps_hbm.1, ...), custom_call_target="tpu_custom_call" | custom-call | tf_op jit(solution)/shard_map/pallas_call | solution.py:626
  41.7 0.6 %shard_map.132 = (bf16[24,512]{1,0:T(8,128)(2,1)}, bf16[24,512]{1,0:T(8,128)(2,1)}) custom-call(bf16[24,512]{1,0:T(8,128)(2,1)S(1)} %get-tuple-element.4.attended_in, bf16[24,512]{1,0:T(8,128)(2,1)S(1)} %get-tuple-element.5.layer_in), custom_call_target="tpu_custom_call" | custom-call | tf_op jit(solution)/shard_map/pallas_call | solution.py:699

commit v11 on v10

--- a/solution.py
+++ b/solution.py
@@ -24,6 +24,10 @@
     centered = values - mean
     var = jnp.mean(centered * centered, axis=-1, keepdims=True)
     return centered / jnp.sqrt(var + 1e-05) * gain
+
+
+def key_groups(side):
+    return {8: ([2, 6, 0], [1, 7], [3, 5, 4]), 4: ([0], [1], [3, 2])}[side]
 
 
 def matmul(a, b):
@@ -77,17 +81,23 @@
     head_recv,
     kv_all,
     near_wide,
+    next_wide,
     far_wide,
     near_keys,
+    next_keys,
     far_keys,
     q_all,
     near_scores,
+    next_scores,
     far_scores,
     near_weights,
+    next_weights,
     far_weights,
+    first_mixed,
+    next_mixed,
+    first_tops,
+    next_tops,
     far_tops,
-    first_mixed,
-    first_tops,
     part_send,
     part_recv,
     ctx_send,
@@ -312,7 +322,7 @@
                 relay.start()
 
     slots = [0] + near
-    near_count = near_wide.shape[0] // block
+    near_count = side // 2 + 1
 
     def wait_for(line, wanted):
         for slot, copy, onward in line:
@@ -381,26 +391,39 @@
 
     steps = side // 2
     pairs = [tuple(slots[2 * step : 2 * step + 2]) for step in range(steps)]
-    near_order = [2, 6, 1, 7, 0] if side == 8 else slots[:near_count]
-    far_order = slots[near_count:]
+    near_order, next_order, far_order = key_groups(side)
+    ahead = min(2, steps)
     wait_for(q_line, slots[:near_count])
     lay_out_line(near_order, near_wide, near_keys)
 
-    @pl.loop(0, max(steps // 2, 1))
+    def scored(step, keys):
+        query = [unfolded(chosen(2 * step + j, slots)) for j in range(2)]
+        return matmul(jnp.concatenate(query, axis=0), keys[...])
+
+    @pl.loop(0, steps // ahead)
     def _(turn):
         @pl.when(turn == steps // 4)
         def _():
-            wait_for(q_line, far_order)
-
-        ahead = min(2, steps)
+            wait_for(q_line, slots[near_count:])
+
         for i in range(ahead):
-            step = ahead * turn + i
-            query = [unfolded(chosen(2 * step + j, slots)) for j in range(2)]
-            near_scores[i] = matmul(jnp.concatenate(query, axis=0), near_keys[...])
+            near_scores[i] = scored(ahead * turn + i, near_keys)
         for i in range(ahead):
             step = ahead * turn + i
             soften(near_scores.at[i], near_weights.at[i], first_tops.at[step])
             first_mixed[step] = matmul(near_weights[i], near_wide[...])
+
+    lay_out_line(next_order, next_wide, next_keys)
+
+    @pl.loop(0, steps // ahead)
+    def _(turn):
+        for i in range(ahead):
+            next_scores[i] = scored(ahead * turn + i, next_keys)
+        for i in range(ahead):
+            step = ahead * turn + i
+            soften(next_scores.at[i], next_weights.at[i], next_tops.at[step], first_tops.at[step])
+            mixed = first_mixed[step] * jnp.exp2(first_tops[step] - next_tops[step])
+            next_mixed[step] = mixed + matmul(next_weights[i], next_wide[...])
 
     lay_out_line(far_order, far_wide, far_keys)
 
@@ -418,14 +441,14 @@
         query = jnp.concatenate([unfolded(d) for d in pairs[step]], axis=0)
         far_scores[step] = matmul(query, far_keys[...])
 
-    turns = [1, 3, 2, 0] if side == 8 else list(range(steps))[::-1]
+    turns = list(range(steps))[::-1]
     score_far(turns[0])
     for step, following_step in zip(turns, turns[1:] + [None]):
         if following_step is not None:
             score_far(following_step)
-        soften(far_scores.at[step], far_weights.at[step], far_tops.at[step], first_tops.at[step])
+        soften(far_scores.at[step], far_weights.at[step], far_tops.at[step], next_tops.at[step])
         top = far_tops[step]
-        mixed = first_mixed[step] * jnp.exp2(first_tops[step] - top)
+        mixed = next_mixed[step] * jnp.exp2(next_tops[step] - top)
         mixed = mixed + matmul(far_weights[step], far_wide[...])
         for i in (1, 0):
             d = pairs[step][i]
@@ -617,8 +640,7 @@
     groups = lax.axis_size("kv")
     side = math.isqrt(lax.axis_size("tm"))
     block = rows * groups
-    near_rows = (5 if side == 8 else side // 2) * block
-    far_rows = side * block - near_rows
+    near_rows, next_rows, far_rows = [len(group) * block for group in key_groups(side)]
     part_rows = block // 2 + -(-2 * side * -(-block // LANES) // HALO) * HALO
     vmem = pl.BlockSpec(memory_space=pltpu.VMEM)
     anywhere = pl.BlockSpec(memory_space=pl.ANY)
@@ -642,14 +664,20 @@
             pltpu.VMEM((groups, 2 * rows, LANES), BF16),
             pltpu.VMEM((side, block, LANES), BF16),
             pltpu.VMEM((near_rows, LANES), BF16),
+            pltpu.VMEM((next_rows, LANES), BF16),
             pltpu.VMEM((far_rows, LANES), BF16),
             pltpu.VMEM((LANES, near_rows), BF16),
+            pltpu.VMEM((LANES, next_rows), BF16),
             pltpu.VMEM((LANES, far_rows), BF16),
             pltpu.VMEM((side, block // 2, LANES), BF16),
             pltpu.VMEM((2, 2 * block, near_rows), F32),
+            pltpu.VMEM((2, 2 * block, next_rows), F32),
             pltpu.VMEM((side // 2, 2 * block, far_rows), F32),
             pltpu.VMEM((2, 2 * block, near_rows), BF16),
+            pltpu.VMEM((2, 2 * block, next_rows), BF16),
             pltpu.VMEM((side // 2, 2 * block, far_rows), BF16),
+            pltpu.VMEM((side // 2, 2 * block, LANES), F32),
+            pltpu.VMEM((side // 2, 2 * block, LANES), F32),
             pltpu.VMEM((side // 2, 2 * block, LANES), F32),
             pltpu.VMEM((side // 2, 2 * block, LANES), F32),
             pltpu.VMEM((side // 2, 2 * block, LANES), F32),

time: 42.5 us -> 43.5 us (1.024)
  Pallas kernels: 41.7 us -> 42.7 us
    pallas_call x1, Pallas kernels: 41.1 us -> 42 us  [on_device(): pl.pallas_call(functools.partial(layer_kernel, side), out_shape=(pltpu.VM...]
where the time goes in v11:
time: 43.5 us; the launch traced here: 43.3 us
  Pallas kernels  42.7 us (98%)
  between operations  0.64 us (1%)
    pallas_call x1, Pallas kernels, on_device(): pl.pallas_call(functools.partial(layer_kernel, side), out_shape=(pltpu.VM...  42 us

profile of v11, /device:TPU:1, one launch (start us, length us, event | category | flops | bytes accessed | tf_op | source)
XLA Modules:
  0.0 43.3 jit_solution(14966064079951067320)
XLA Ops:
  0.6 42.0 %shard_map.131 = (bf16[24,512]{1,0:T(8,128)(2,1)S(1)}, bf16[24,512]{1,0:T(8,128)(2,1)S(1)}) custom-call(bf16[24,512]{1,0:T(8,128)(2,1)} %frames_hbm.1, f32[1,512]{1,0:T(1,128)} %bitcast.4, f32[1,512]{1,0:T(1,128)} %bitcast.5, f32[1,512]{1,0:T(1,128)} %bitcast.6, f32[1,512]{1,0:T(1,128)} %bitcast.7, f32[31,512]{1,0:T(8,128)} %taps_hbm.1, ...), custom_call_target="tpu_custom_call" | custom-call | tf_op jit(solution)/shard_map/pallas_call | solution.py:648
  42.7 0.6 %shard_map.132 = (bf16[24,512]{1,0:T(8,128)(2,1)}, bf16[24,512]{1,0:T(8,128)(2,1)}) custom-call(bf16[24,512]{1,0:T(8,128)(2,1)S(1)} %get-tuple-element.4.attended_in, bf16[24,512]{1,0:T(8,128)(2,1)S(1)} %get-tuple-element.5.layer_in), custom_call_target="tpu_custom_call" | custom-call | tf_op jit(solution)/shard_map/pallas_call | solution.py:727

commit v12 on v9

--- a/solution.py
+++ b/solution.py
@@ -280,18 +280,18 @@
             return [entry(d, whole) for d in near]
         if halved:
             return [
+                entry(1, whole),
+                entry(7, whole),
                 entry(2, lower, [(4, lower, 2), (3, lower, 1)]),
                 entry(6, upper, [(4, upper, 6), (5, upper, 7)]),
                 entry(2, upper, [(3, upper, 1)]),
                 entry(6, lower, [(5, lower, 7)]),
-                entry(1, whole),
-                entry(7, whole),
             ]
         return [
+            entry(1, whole),
+            entry(7, whole),
             entry(2, whole, [(4, lower, 2), (3, whole, 1)]),
             entry(6, whole, [(4, upper, 6), (5, whole, 7)]),
-            entry(1, whole),
-            entry(7, whole),
         ]
 
     kv_line = line_copies(kv_all, kv_ssem, kv_rsem, key_peer, True)
@@ -370,12 +370,11 @@
             high = line.astype(BF16).astype(F32)
             levels = jnp.where(place == i, high, levels)
             levels = jnp.where(place == level_rows + i, line - high, levels)
-        part_send[d] = jnp.concatenate(
-            [folded(mixed / total), levels], axis=0
-        ).astype(BF16)
-
-    def chosen(step, order):
-        return sum((step == i).astype(jnp.int32) * d for i, d in enumerate(order))
+        part = jnp.concatenate([folded(mixed / total), levels], axis=0).astype(BF16)
+        if d > 0:
+            part_send[d] = part
+        else:
+            part_recv[d] = part
 
     steps = side // 2
     pairs = [tuple(slots[2 * step : 2 * step + 2]) for step in range(steps)]
@@ -384,21 +383,19 @@
     wait_for(q_line, slots[:near_count])
     lay_out_line(near_order, near_wide, near_keys)
 
-    @pl.loop(0, max(steps // 2, 1))
-    def _(turn):
-        @pl.when(turn == steps // 4)
-        def _():
+    def score_near(step):
+        if step == near_count // 2:
             wait_for(q_line, far_order)
-
-        ahead = min(2, steps)
-        for i in range(ahead):
-            step = ahead * turn + i
-            query = [unfolded(chosen(2 * step + j, slots)) for j in range(2)]
-            near_scores[i] = matmul(jnp.concatenate(query, axis=0), near_keys[...])
-        for i in range(ahead):
-            step = ahead * turn + i
-            soften(near_scores.at[i], near_weights.at[i], first_tops.at[step])
-            first_mixed[step] = matmul(near_weights[i], near_wide[...])
+        query = jnp.concatenate([unfolded(d) for d in pairs[step]], axis=0)
+        near_scores[step & 1] = matmul(query, near_keys[...])
+
+    score_near(0)
+    for step in range(steps):
+        if step + 1 < steps:
+            score_near(step + 1)
+        i = step & 1
+        soften(near_scores.at[i], near_weights.at[i], first_tops.at[step])
+        first_mixed[step] = matmul(near_weights[i], near_wide[...])
 
     lay_out_line(far_order, far_wide, far_keys)
 
@@ -431,7 +428,6 @@
             if d > 0:
                 part_copy(d).start()
 
-    part_recv[0] = part_send[0]
     for d in range(1, side):
         part_copy(d).wait_recv()
 

time: 41.8 us -> 42.8 us (1.024)
  Pallas kernels: 41 us -> 42 us
    pallas_call x1, Pallas kernels: 40.3 us -> 41.4 us  [on_device(): pl.pallas_call(functools.partial(layer_kernel, side), out_shape=(pltpu.VM...]
where the time goes in v12:
time: 42.8 us; the launch traced here: 42.7 us
  Pallas kernels  42 us (98%)
  between operations  0.64 us (1%)
    pallas_call x1, Pallas kernels, on_device(): pl.pallas_call(functools.partial(layer_kernel, side), out_shape=(pltpu.VM...  41.4 us

profile of v12, /device:TPU:1, one launch (start us, length us, event | category | flops | bytes accessed | tf_op | source)
XLA Modules:
  0.0 42.7 jit_solution(7644798523456899222)
XLA Ops:
  0.6 41.4 %shard_map.131 = (bf16[24,512]{1,0:T(8,128)(2,1)S(1)}, bf16[24,512]{1,0:T(8,128)(2,1)S(1)}) custom-call(bf16[24,512]{1,0:T(8,128)(2,1)} %frames_hbm.1, f32[1,512]{1,0:T(1,128)} %bitcast.4, f32[1,512]{1,0:T(1,128)} %bitcast.5, f32[1,512]{1,0:T(1,128)} %bitcast.6, f32[1,512]{1,0:T(1,128)} %bitcast.7, f32[31,512]{1,0:T(8,128)} %taps_hbm.1, ...), custom_call_target="tpu_custom_call" | custom-call | tf_op jit(solution)/shard_map/pallas_call | solution.py:624
  42.0 0.6 %shard_map.132 = (bf16[24,512]{1,0:T(8,128)(2,1)}, bf16[24,512]{1,0:T(8,128)(2,1)}) custom-call(bf16[24,512]{1,0:T(8,128)(2,1)S(1)} %get-tuple-element.4.attended_in, bf16[24,512]{1,0:T(8,128)(2,1)S(1)} %get-tuple-element.5.layer_in), custom_call_target="tpu_custom_call" | custom-call | tf_op jit(solution)/shard_map/pallas_call | solution.py:697

commit v13 on v9

--- a/solution.py
+++ b/solution.py
@@ -304,12 +304,11 @@
     ).astype(BF16)
     for _, copy, _ in q_line:
         copy.start()
-    for line in (q_line, kv_line):
-        for _, copy, onward in line:
-            if onward:
-                copy.wait_recv()
-            for _, relay in onward:
-                relay.start()
+    for _, copy, onward in kv_line[:2] + q_line + kv_line[2:]:
+        if onward:
+            copy.wait_recv()
+        for _, relay in onward:
+            relay.start()
 
     slots = [0] + near
     near_count = near_wide.shape[0] // block

time: 41.8 us -> 42.2 us (level)
  Pallas kernels: 41 us -> 41.5 us
    pallas_call x1, Pallas kernels: 40.3 us -> 40.8 us  [on_device(): pl.pallas_call(functools.partial(layer_kernel, side), out_shape=(pltpu.VM...]
where the time goes in v13:
time: 42.2 us; the launch traced here: 42.1 us
  Pallas kernels  41.5 us (98%)
  between operations  0.64 us (2%)
    pallas_call x1, Pallas kernels, on_device(): pl.pallas_call(functools.partial(layer_kernel, side), out_shape=(pltpu.VM...  40.8 us

profile of v13, /device:TPU:1, one launch (start us, length us, event | category | flops | bytes accessed | tf_op | source)
XLA Modules:
  0.0 42.1 jit_solution(85044048156730355)
XLA Ops:
  0.6 40.8 %shard_map.131 = (bf16[24,512]{1,0:T(8,128)(2,1)S(1)}, bf16[24,512]{1,0:T(8,128)(2,1)S(1)}) custom-call(bf16[24,512]{1,0:T(8,128)(2,1)} %frames_hbm.1, f32[1,512]{1,0:T(1,128)} %bitcast.4, f32[1,512]{1,0:T(1,128)} %bitcast.5, f32[1,512]{1,0:T(1,128)} %bitcast.6, f32[1,512]{1,0:T(1,128)} %bitcast.7, f32[31,512]{1,0:T(8,128)} %taps_hbm.1, ...), custom_call_target="tpu_custom_call" | custom-call | tf_op jit(solution)/shard_map/pallas_call | solution.py:627
  41.5 0.6 %shard_map.132 = (bf16[24,512]{1,0:T(8,128)(2,1)}, bf16[24,512]{1,0:T(8,128)(2,1)}) custom-call(bf16[24,512]{1,0:T(8,128)(2,1)S(1)} %get-tuple-element.4.attended_in, bf16[24,512]{1,0:T(8,128)(2,1)S(1)} %get-tuple-element.5.layer_in), custom_call_target="tpu_custom_call" | custom-call | tf_op jit(solution)/shard_map/pallas_call | solution.py:700

commit v14 on v9

--- a/solution.py
+++ b/solution.py
@@ -381,8 +381,8 @@
     pairs = [tuple(slots[2 * step : 2 * step + 2]) for step in range(steps)]
     near_order = [2, 6, 1, 7, 0] if side == 8 else slots[:near_count]
     far_order = slots[near_count:]
+    lay_out_line(near_order, near_wide, near_keys)
     wait_for(q_line, slots[:near_count])
-    lay_out_line(near_order, near_wide, near_keys)
 
     @pl.loop(0, max(steps // 2, 1))
     def _(turn):

time: 41.8 us -> 41.8 us (level)
  no operation moved by 1% of the time
where the time goes in v14:
time: 41.8 us; the launch traced here: 41.6 us
  Pallas kernels  41 us (98%)
  between operations  0.64 us (2%)
    pallas_call x1, Pallas kernels, on_device(): pl.pallas_call(functools.partial(layer_kernel, side), out_shape=(pltpu.VM...  40.3 us

profile of v14, /device:TPU:1, one launch (start us, length us, event | category | flops | bytes accessed | tf_op | source)
XLA Modules:
  0.0 41.6 jit_solution(12338612253635883835)
XLA Ops:
  0.6 40.3 %shard_map.131 = (bf16[24,512]{1,0:T(8,128)(2,1)S(1)}, bf16[24,512]{1,0:T(8,128)(2,1)S(1)}) custom-call(bf16[24,512]{1,0:T(8,128)(2,1)} %frames_hbm.1, f32[1,512]{1,0:T(1,128)} %bitcast.4, f32[1,512]{1,0:T(1,128)} %bitcast.5, f32[1,512]{1,0:T(1,128)} %bitcast.6, f32[1,512]{1,0:T(1,128)} %bitcast.7, f32[31,512]{1,0:T(8,128)} %taps_hbm.1, ...), custom_call_target="tpu_custom_call" | custom-call | tf_op jit(solution)/shard_map/pallas_call | solution.py:628
  41.0 0.6 %shard_map.132 = (bf16[24,512]{1,0:T(8,128)(2,1)}, bf16[24,512]{1,0:T(8,128)(2,1)}) custom-call(bf16[24,512]{1,0:T(8,128)(2,1)S(1)} %get-tuple-element.4.attended_in, bf16[24,512]{1,0:T(8,128)(2,1)S(1)} %get-tuple-element.5.layer_in), custom_call_target="tpu_custom_call" | custom-call | tf_op jit(solution)/shard_map/pallas_call | solution.py:701
